TPU v7x, 256 devices: a whole 4x4x8 slice. The times are simulated.
256 devices in a mesh: section: 2 (over core), wide: 32 (over z_lo, y, x), narrow: 4 (over z_hi).
Axes of the slice: x: 4, y: 4, z: 8 (z_hi: 4, z_lo: 2; z = z_hi * 2 + z_lo), core: 2. Of those that a mesh axis runs over, the one named last changes fastest.
Arguments:
- teacher_rows: bfloat16 [24576, 6656], P(('section', 'wide'), 'narrow'), may hold values from -150 to 150, as said below
- teacher_gain: bfloat16 [6656], P('narrow'), may hold values from 0.5 to 1.5
- projector: bfloat16 [6656, 3072], P('narrow', 'wide'), may hold values from -0.078125 to 0.078125
- student_rows: bfloat16 [24576, 3072], P(('section', 'wide'), 'narrow'), may hold values from -16 to 16
- student_weight: bfloat16 [3072, 3072], P(None, 'narrow'), may hold values from -0.109375 to 0.109375
Outputs:
- input_grad: bfloat16 [24576, 3072], P(('section', 'wide'), 'narrow')
- weight_grad: float32 [3072, 3072], P(('section', 'wide'), 'narrow')
Inputs may be any that keep to these rules, and one draw needn't show every extreme that they name: teacher_rows have row scales and feature scales that differ.
All inputs are finite; a program needn't handle non-finite values.
Results may differ from a plain program's by a relative error of at most 0.015.
Values may be sent and summed in bfloat16 or wider, within the bound.
A program may use at most 128 MiB of HBM per device.

v0:
```python
import jax
import jax.numpy as jnp
from jax import lax
from jax.sharding import PartitionSpec as P


def swapped(block, axis, stride):
    count = lax.axis_size(axis)
    route = []
    for low in range(count):
        high = low | 1 << stride
        if high != low and high < count:
            route += [(low, high), (high, low)]
    return lax.ppermute(block, axis, route)


def project_rows(feed, projector):
    regrouped = jnp.dot(
        feed,
        lax.all_gather(projector, "wide", axis=1, tiled=True),
        preferred_element_type=jnp.float32,
    ).astype(jnp.bfloat16)
    summed = lax.psum_scatter(
        regrouped.astype(jnp.float32).astype(jnp.bfloat16),
        "narrow",
        scatter_dimension=1,
        tiled=True,
    )
    return summed


def shards(teacher_rows, teacher_gain, projector, student_rows, student_weight):
    teacher_f32 = teacher_rows.astype(jnp.float32)
    local_squares = jnp.sum(teacher_f32 * teacher_f32, axis=1)
    total_squares = lax.psum(local_squares, "narrow")
    feature_count = teacher_rows.shape[1] * lax.axis_size("narrow")
    inverse_rms = lax.rsqrt(total_squares / feature_count + 1e-05)
    hidden = (
        teacher_f32 * inverse_rms[:, None] * teacher_gain.astype(jnp.float32)[None, :]
    ).astype(jnp.bfloat16)
    paired = swapped(hidden, "section", 0)
    target = project_rows(paired, projector)
    full_rows = lax.all_gather(student_rows, "narrow", axis=1, tiled=True)
    output = student_rows.astype(jnp.float32) + jnp.dot(
        full_rows, student_weight, preferred_element_type=jnp.float32
    )
    mismatch = (output - target.astype(jnp.float32)).astype(jnp.bfloat16)
    back_terms = lax.dot_general(
        mismatch, student_weight, (((1,), (1,)), ((), ())), preferred_element_type=jnp.float32
    ).astype(jnp.bfloat16)
    back_sum = lax.psum_scatter(
        back_terms.astype(jnp.float32).astype(jnp.bfloat16),
        "narrow",
        scatter_dimension=1,
        tiled=True,
    ).astype(jnp.float32)
    input_grad = (mismatch.astype(jnp.float32) + back_sum).astype(jnp.bfloat16)
    token_count = student_rows.shape[0] * lax.axis_size("section") * lax.axis_size("wide")
    grad_term = lax.dot_general(
        full_rows, mismatch, (((0,), (0,)), ((), ())), preferred_element_type=jnp.float32
    ) / jnp.sqrt(jnp.float32(token_count))
    weight_grad = lax.psum_scatter(grad_term, ("section", "wide"), scatter_dimension=0, tiled=True)
    return (input_grad, weight_grad)


def solution(mesh):
    placed = (
        P(("section", "wide"), "narrow"),
        P("narrow"),
        P("narrow", "wide"),
        P(("section", "wide"), "narrow"),
        P(None, "narrow"),
    )
    return jax.shard_map(
        shards,
        mesh=mesh,
        in_specs=placed,
        out_specs=(P(("section", "wide"), "narrow"), P(("section", "wide"), "narrow")),
        check_vma=False,
    )
```

profile of v0, /device:TPU:32, one launch (start us, length us, event | category | flops | bytes accessed | tf_op | source)
XLA Modules:
  0.0 700.8 jit_solution(4283873929822581855)
XLA Ops:
  7.2 0.0 copy-start
  7.2 0.0 all-gather.5.cloned.1.call-start
  7.2 0.7 all-gather.5.cloned.1.call-update
  7.9 0.0 all-gather.3.cloned.1.call-start
  8.0 0.7 all-gather.3.cloned.1.call-update
  8.7 0.0 reduce-scatter.6.cloned.1.call-start
  8.7 0.7 convert_element_type.39
  9.4 1.6 fusion
  11.0 14.1 %psum.7 = f32[384]{0:T(512)S(1)} all-reduce(f32[384]{0:T(512)S(1)} %fusion), channel_id=1, replica_groups=mesh['section'=2,'wide'=32,'narrow'=4] {'narrow'}, use_global_device_ids=true, to_apply=%region_1.0 | all-reduce | flops 384 | bytes 3072 | tf_op jit(solution)/shard_map/psum | solution.py:35
  25.2 0.0 copy-done
  25.2 0.4 fusion.2
  25.5 0.1 collective-permute-start
  25.6 3.0 collective-permute-done
  28.6 156.4 %all-gather.5.cloned.1.call-done = bf16[1664,3072]{0,1:T(8,128)(2,1)} async-done(((bf16[1664,96]{0,1:T(8,128)(2,1)}), bf16[1664,3072]{0,1:T(8,128)(2,1)}) %all-gather.5.cloned.1.call-update) | async-done | bytes 10223632 | tf_op jit(solution)/shard_map/all_gather | solution.py:20
  185.0 11.9 %convolution_convert_fusion.1 = bf16[384,3072]{1,0:T(8,128)(2,1)} fusion(bf16[384,1664]{1,0:T(8,128)(2,1)S(1)} %collective-permute-done, bf16[1664,3072]{0,1:T(8,128)(2,1)} %all-gather.5.cloned.1.call-done), kind=kOutput, calls=%fused_computation.2 | convolution fusion | flops 3927048192 | bytes 13860864 | tf_op jit(solution)/shard_map/dot_general | solution.py:18
  196.9 0.0 copy-start.2
  196.9 0.0 reduce-scatter.6.cloned.1.call-update
  197.0 0.0 reduce-scatter.8.cloned.1.call-start
  197.0 46.4 %all-gather.3.cloned.1.call-done = bf16[384,3072]{1,0:T(8,128)(2,1)} async-done(((bf16[384,768]{1,0:T(8,128)(2,1)}), bf16[384,3072]{1,0:T(8,128)(2,1)}) %all-gather.3.cloned.1.call-update) | async-done | bytes 2359312 | tf_op jit(solution)/shard_map/all_gather | solution.py:43
  243.5 0.0 copy-done.2
  243.5 5.0 convolution_add_fusion
  248.5 47.8 %reduce-scatter.6.cloned.1.call-done = bf16[384,768]{1,0:T(8,128)(2,1)} async-done(((bf16[384,3072]{1,0:T(8,128)(2,1)}), bf16[384,768]{1,0:T(8,128)(2,1)}) %reduce-scatter.6.cloned.1.call-update) | async-done | bytes 589840 | tf_op jit(solution)/shard_map/reduce_scatter | solution.py:23
  296.4 1.2 subtract_convert_fusion
  297.5 5.8 convolution_convert_fusion
  303.3 0.0 copy-start.1
  303.3 0.0 reduce-scatter.8.cloned.1.call-update
  303.3 0.0 reduce-scatter.10.cloned.1.call-start
  303.4 1.6 copy-done.1
  305.0 5.0 multiply_bitcast_fusion
  310.0 9.7 %copy.9 = f32[3072,768]{1,0:T(8,128)} copy(f32[3072,768]{0,1:T(8,128)} %multiply_bitcast_fusion) | data formatting | bytes 18874368
  319.7 0.0 reduce-scatter.10.cloned.1.call-update
  319.8 36.8 %reduce-scatter.8.cloned.1.call-done = bf16[384,768]{1,0:T(8,128)(2,1)} async-done(((bf16[384,3072]{1,0:T(8,128)(2,1)}), bf16[384,768]{1,0:T(8,128)(2,1)}) %reduce-scatter.8.cloned.1.call-update) | async-done | bytes 589840 | tf_op jit(solution)/shard_map/reduce_scatter | solution.py:51
  356.5 2.0 add_convert_fusion
  358.5 335.8 %reduce-scatter.10.cloned.1.call-done = f32[48,768]{1,0:T(8,128)} async-done(((f32[3072,768]{1,0:T(8,128)}), f32[48,768]{1,0:T(8,128)}) %reduce-scatter.10.cloned.1.call-update) | async-done | bytes 147472
  (1 shorter events, 0.0 us)
Async XLA Ops:
  7.2 18.0 %copy-start = (bf16[384,1664]{1,0:T(8,128)(2,1)S(1)}, bf16[384,1664]{1,0:T(8,128)(2,1)}, u32[]{:S(2)}) copy-start(bf16[384,1664]{1,0:T(8,128)(2,1)} %param.5) | copy-start | bytes 3833860
  7.2 177.8 %all-gather.5.cloned.1.call-start = ((), (), s32[]{:S(2)}) async-start(), calls=%async_computation.4 | async-start | bytes 10543104 | tf_op jit(solution)/shard_map/all_gather | solution.py:20
  7.9 235.5 %all-gather.3.cloned.1.call-start = ((), (), s32[]{:S(2)}) async-start(), calls=%async_computation.3 | async-start | bytes 2949120 | tf_op jit(solution)/shard_map/all_gather | solution.py:43
  8.7 287.7 %reduce-scatter.6.cloned.1.call-start = ((), (), s32[]{:S(2)}) async-start(), calls=%async_computation.5 | async-start | bytes 2949120 | tf_op jit(solution)/shard_map/reduce_scatter | solution.py:23
  25.5 3.1 collective-permute-start
  196.9 46.5 %copy-start.2 = (bf16[384,768]{1,0:T(8,128)(2,1)S(1)}, bf16[384,768]{1,0:T(8,128)(2,1)}, u32[]{:S(2)}) copy-start(bf16[384,768]{1,0:T(8,128)(2,1)} %param.8) | copy-start | bytes 1769476
  197.0 159.6 %reduce-scatter.8.cloned.1.call-start = ((), (), s32[]{:S(2)}) async-start(), calls=%async_computation.6 | async-start | bytes 2949120 | tf_op jit(solution)/shard_map/reduce_scatter | solution.py:51
  303.3 1.7 copy-start.1
  303.3 391.0 %reduce-scatter.10.cloned.1.call-start = ((), (), s32[]{:S(2)}) async-start(), calls=%async_computation.7 | async-start | bytes 9584640
Sparse Core Ops, SparseCore 0:
  9.8 175.1 all-gather.4
  186.8 56.6 all-gather.2
  246.0 50.2 reduce-scatter.5
  303.4 53.0 reduce-scatter.7
  359.5 334.7 reduce-scatter.9
where the time goes:
time: 701 us
  waiting for transfers between devices  628 us (90%)
  matrix products  27.8 us (4%)
  blocking collectives  14.1 us (2%)
  between operations  13.8 us (2%)
  local copies, waits for them, and re-layouts  11.3 us (2%)
    unnamed x6, waiting for transfers between devices  337 us
    all_gather x1, waiting for transfers between devices, project_rows(): lax.all_gather(projector, 'wide', axis=1, tiled=True)  156 us
    reduce_scatter x1, waiting for transfers between devices, project_rows(): lax.psum_scatter(regrouped.astype(jnp.float32).astype(jnp.bfloat16), 'nar...  47.8 us
    all_gather x1, waiting for transfers between devices, shards(): full_rows = lax.all_gather(student_rows, 'narrow', axis=1, tiled=True)  46.4 us
    reduce_scatter x1, waiting for transfers between devices, shards(): lax.psum_scatter(back_terms.astype(jnp.float32).astype(jnp.bfloat16), 'na...  36.8 us
    psum x1, blocking collectives, shards(): total_squares = lax.psum(local_squares, 'narrow')  14.1 us
  transfers between devices with their start and end apart: 6, of which 6 were waited for; matrix products, arithmetic and copies ran while one was open for 5% of the time, Pallas kernels for 0%

commit v1 on v0

v1 whole, which is shorter than its diff:
```python
import functools

import jax
import jax.numpy as jnp
from jax import lax
from jax.experimental import pallas as pl
from jax.experimental.pallas import tpu as pltpu
from jax.sharding import PartitionSpec as P

MESH = pl.DeviceIdType.MESH
F32 = jnp.float32
BF16 = jnp.bfloat16

GATHER = 0
ZSWAP = 40
WSEND = 41
WRECV = 44
SQUARES = 45
PAIRED = 48
SIBLING = 49
NARROW_RS = 50
NARROW_AG = 56
CORE_SUM = 62
WIDE_RS = 66
ZSUM = 90
FINAL = 91
SLOTS = 92


class Ring:
    def __init__(self, copy, base, out, opp_in, left_in, right_in, right, left):
        self.out, self.opp_in, self.left_in, self.right_in = out, opp_in, left_in, right_in
        self.copies = [
            copy(out.at[0, 0], opp_in.at[0], base + 0, right),
            copy(out.at[0, 1], opp_in.at[1], base + 1, left),
            copy(out.at[1, 1], left_in.at[1], base + 2, right),
            copy(out.at[2, 0], right_in.at[0], base + 3, left),
            copy(out.at[1, 0], left_in.at[0], base + 4, right),
            copy(out.at[2, 1], right_in.at[1], base + 5, left),
        ]

    def send_far(self, load):
        for h in range(2):
            self.out[0, h] = load(h).astype(BF16)
            self.copies[h].start()

    def send_right_early(self, load):
        self.out[1, 1] = load(1).astype(BF16)
        self.copies[2].start()

    def send_left_early(self, load):
        self.out[2, 0] = load(0).astype(BF16)
        self.copies[3].start()

    def send_right_late(self, load):
        self.copies[0].wait_recv()
        self.out[1, 0] = (load(0) + self.opp_in[0].astype(F32)).astype(BF16)
        self.copies[4].start()

    def send_left_late(self, load):
        self.copies[1].wait_recv()
        self.out[2, 1] = (load(1) + self.opp_in[1].astype(F32)).astype(BF16)
        self.copies[5].start()

    def wait_half(self, h):
        if h == 0:
            self.copies[3].wait_recv()
            self.copies[4].wait_recv()
        else:
            self.copies[2].wait_recv()
            self.copies[5].wait_recv()

    def received(self, h):
        return self.left_in[h].astype(F32) + self.right_in[h].astype(F32)

    def wait_sends(self):
        for item in self.copies:
            item.wait_send()


def kernel(
    t_ref, g_ref, pt_ref, wt_ref, x_ref, xt_ref, ig_ref, wg_ref,
    ct, lhs, hid, sq, part, n_out, n_opp, n_left, n_right, m, igacc,
    gk, core_out, core_in, w_out, w_opp, w_left, w_right, hk, v_out, v_opp, v_left, v_right,
    res, z_out, z_in, fin, send_sem, recv_sem, local_sem,
):
    c = lax.axis_index("section")
    w = lax.axis_index("wide")
    n = lax.axis_index("narrow")
    x, y, zl = w % 4, (w // 4) % 4, w // 16
    tokens, kt = t_ref.shape
    ks = x_ref.shape[1]
    half = pt_ref.shape[0] // 2
    depth = kt + ks
    cut = (depth // 256 + 1) * 128
    cols = ks // 2
    rows = pl.ds(pl.multiple_of(half * c, half), half)

    def at(zz, yy, xx):
        return zz * 16 + yy * 4 + xx

    sibling = {"section": 1 - c}
    x_next, x_prev = {"wide": at(zl, y, (x + 1) % 4)}, {"wide": at(zl, y, (x + 3) % 4)}
    y_next, y_prev = {"wide": at(zl, (y + 1) % 4, x)}, {"wide": at(zl, (y + 3) % 4, x)}
    z_other = {"wide": at(1 - zl, y, x)}
    n_dev = [None] + [{"narrow": (n + d) % 4} for d in (1, 2, 3)]

    target_id = {"section": n // 2, "wide": at(n % 2, y, x), "narrow": (n + 2 * zl + c) % 4}
    own_piece = jnp.logical_and(n == 2 * c + zl, 2 * zl + c == 0)
    from_row = 2 * c + zl
    offset = (n - from_row + 4) % 4
    source_id = {"section": offset % 2, "wide": at(offset // 2, y, x), "narrow": from_row}

    barrier = pltpu.get_barrier_semaphore()
    greeted = [sibling, x_next, x_prev, y_next, y_prev, z_other, n_dev[1], n_dev[2], n_dev[3]]
    for device in greeted:
        pl.semaphore_signal(barrier, inc=1, device_id=device, device_id_type=MESH)

    @pl.when(jnp.logical_not(own_piece))
    def _():
        pl.semaphore_signal(barrier, inc=1, device_id=source_id, device_id_type=MESH)

    pl.semaphore_wait(barrier, jnp.where(own_piece, len(greeted), len(greeted) + 1))

    def copy(src, dst, slot, device):
        return pltpu.make_async_remote_copy(
            src_ref=src, dst_ref=dst, send_sem=send_sem.at[slot], recv_sem=recv_sem.at[slot],
            device_id=device, device_id_type=MESH,
        )

    w_cols = pl.ds(kt, ks)
    w_home = ct.at[w, rows, w_cols]
    owner = w // 8
    w_copies = [
        pltpu.make_async_remote_copy(
            src_ref=wt_ref.at[(n + d) % 4], dst_ref=w_home, send_sem=send_sem.at[WSEND + d - 1],
            recv_sem=recv_sem.at[WRECV], device_id=n_dev[d], device_id_type=MESH,
        )
        for d in (1, 2, 3)
    ]

    @pl.when(n == owner)
    def _():
        for item in w_copies:
            item.start()
        ct[w, rows, w_cols] = wt_ref[n]

    ct[w, rows, pl.ds(0, kt)] = pt_ref[rows, :]

    eye = lax.broadcasted_iota(jnp.int32, (128, 128), 0) == lax.broadcasted_iota(jnp.int32, (128, 128), 1)
    groups = tokens // 128
    sq[0] = jnp.zeros((8, 128), F32)
    for i in range(groups):
        part_t = t_ref[128 * i : 128 * i + 128, :].astype(F32)
        col = jnp.sum(part_t * part_t, axis=1, keepdims=True)
        sq[0, i : i + 1, :] = jnp.sum(jnp.where(eye, col, 0.0), axis=0, keepdims=True)
    sq_copies = [copy(sq.at[0], sq.at[d], SQUARES + d - 1, n_dev[d]) for d in (1, 2, 3)]
    for item in sq_copies:
        item.start()

    @pl.when(n != owner)
    def _():
        w_copies[0].wait_recv()

    def slab(index, part=None):
        if part is None:
            return ct.at[index, rows]
        return ct.at[index, rows, pl.ds(0, cut) if part == 0 else pl.ds(cut, depth - cut)]

    def spread(index, slot, device, part=None):
        return copy(slab(index, part), slab(index, part), slot, device)

    sent = []

    def go(item):
        item.start()
        sent.append(item)

    def to_sibling(index):
        copy(slab(index), slab(index), SIBLING, sibling).start()

    class Family:
        def __init__(self, f):
            self.base = GATHER + 20 * f
            self.f = f
            self.plane = zl if f == 0 else 1 - zl
            self.a, self.b = (x, y) if f == 0 else (y, x)
            self.first = (x_next, x_prev) if f == 0 else (y_next, y_prev)
            self.second = (y_next, y_prev) if f == 0 else (x_next, x_prev)

        def index(self, da, db):
            a, b = (self.a + da) % 4, (self.b + db) % 4
            return at(self.plane, b, a) if self.f == 0 else at(self.plane, a, b)

        def begin(self):
            own = self.index(0, 0)
            go(spread(own, self.base, self.first[0]))
            go(spread(own, self.base + 1, self.first[1]))
            self.second_send(0)
            to_sibling(own)

        ALONG = (0, 3, 1, 2)

        def second_send(self, j):
            index = self.index(self.ALONG[j], 0)
            go(spread(index, self.base + 4 + 4 * j, self.second[0]))
            go(spread(index, self.base + 5 + 4 * j, self.second[1]))

        def first_near(self):
            for side in range(2):
                index = self.index(self.ALONG[1 + side], 0)
                spread(index, self.base + side, self.first[side]).wait_recv()
                go(spread(index, self.base + 2 + side, self.first[side], side))
                self.second_send(1 + side)
                to_sibling(index)

        def first_far(self):
            index = self.index(2, 0)
            for side in range(2):
                spread(index, self.base + 2 + side, self.first[side], side).wait_recv()
            self.second_send(3)
            to_sibling(index)

        def second_near(self, j):
            slot = self.base + 4 + 4 * j
            for side in range(2):
                index = self.index(self.ALONG[j], 3 if side == 0 else 1)
                spread(index, slot + side, self.second[side]).wait_recv()
                go(spread(index, slot + 2 + side, self.second[side], side))
                to_sibling(index)

        def second_far(self, j):
            slot = self.base + 4 + 4 * j
            index = self.index(self.ALONG[j], 2)
            for side in range(2):
                spread(index, slot + 2 + side, self.second[side], side).wait_recv()
            to_sibling(index)

    fams = [Family(0), Family(1)]
    z_copy = spread(w, ZSWAP, z_other)
    go(z_copy)
    fams[0].begin()

    lhs[:, kt:] = x_ref[...]
    for item in sq_copies:
        item.wait_recv()
    inverse = lax.rsqrt((sq[0] + sq[1] + sq[2] + sq[3]) / (4 * kt) + 1e-05)
    gain = g_ref[...].astype(F32)
    for i in range(groups):
        col = jnp.sum(jnp.where(eye, inverse[i : i + 1, :], 0.0), axis=1, keepdims=True)
        span = slice(128 * i, 128 * i + 128)
        hid[span, :] = -(t_ref[span, :].astype(F32) * col * gain).astype(BF16)
    paired_copy = copy(hid, lhs.at[:, pl.ds(0, kt)], PAIRED, sibling)
    go(paired_copy)

    z_copy.wait_recv()
    fams[1].begin()
    for fam in fams:
        fam.first_near()
    for fam in fams:
        fam.second_near(0)
    for fam in fams:
        fam.first_far()
    for j in (1, 2, 3):
        for fam in fams:
            fam.second_near(j)
            fam.second_far(j - 1)
    for fam in fams:
        fam.second_far(3)
    all_half = ct.at[:, rows]
    sibling_all = copy(all_half, all_half, SIBLING, sibling)
    sibling_all.wait_recv()
    paired_copy.wait_recv()

    ring = Ring(copy, NARROW_RS, n_out, n_opp, n_left, n_right, n_dev[1], n_dev[3])

    def product(i, carry):
        r, h = i // 2, i % 2
        d = jnp.where(r == 0, 2, jnp.where(r == 1, 1, jnp.where(r == 2, 3, 0)))
        b = (n + d) % 4
        block = ct[pl.ds(8 * b + 4 * h, 4)].reshape(cols, depth)
        part[r, h] = lax.dot_general(
            lhs[...], block, (((1,), (1,)), ((), ())), preferred_element_type=F32
        )

        @pl.when(i == 1)
        def _():
            ring.send_far(lambda k: part[0, k])

        @pl.when(i == 3)
        def _():
            ring.send_right_early(lambda k: part[1, k])

        @pl.when(i == 5)
        def _():
            ring.send_left_early(lambda k: part[2, k])

        return carry

    lax.fori_loop(0, 8, product, 0)
    ring.send_right_late(lambda k: part[1, k])
    ring.send_left_late(lambda k: part[2, k])

    ag = [
        copy(m.at[n, 0], m.at[n, 0], NARROW_AG, n_dev[1]),
        copy(m.at[n, 1], m.at[n, 1], NARROW_AG + 1, n_dev[1]),
        copy(m.at[n, 0], m.at[n, 0], NARROW_AG + 2, n_dev[3]),
        copy(m.at[n, 1], m.at[n, 1], NARROW_AG + 3, n_dev[3]),
        copy(m.at[(n + 3) % 4, 0], m.at[(n + 3) % 4, 0], NARROW_AG + 4, n_dev[1]),
        copy(m.at[(n + 1) % 4, 1], m.at[(n + 1) % 4, 1], NARROW_AG + 5, n_dev[3]),
    ]
    for h in range(2):
        ring.wait_half(h)
        own = part[3, h] + x_ref[:, cols * h : cols * h + cols].astype(F32)
        m[n, h] = (own + ring.received(h)).astype(BF16)
        ag[h].start()
        ag[2 + h].start()

    igacc[...] = jnp.zeros((tokens, ks), F32)

    def core_copy(f, h):
        return copy(core_out.at[f, h], core_in.at[f, h], CORE_SUM + 2 * f + h, sibling)

    def backward(i, carry):
        r, h = i // 2, i % 2

        @pl.when(i == 2)
        def _():
            ag[0].wait_recv()
            ag[4].start()
            ag[3].wait_recv()
            ag[5].start()
            ag[1].wait_recv()

        @pl.when(i == 4)
        def _():
            ag[2].wait_recv()

        @pl.when(i == 6)
        def _():
            ag[4].wait_recv()
            ag[5].wait_recv()

        d = jnp.where(r == 0, 0, jnp.where(r == 1, 3, jnp.where(r == 2, 1, 2)))
        b = (n + d) % 4
        f = d // 2
        piece = m[b, h]
        block = ct[pl.ds(8 * b + 4 * h, 4), :, pl.ds(kt, ks)].reshape(cols, ks)
        igacc[...] += jnp.dot(piece, block, preferred_element_type=F32)
        grad = jnp.dot(xt_ref[...], piece, preferred_element_type=F32)

        @pl.when(c == d % 2)
        def _():
            gk[f, h] = grad.reshape(4, 4, half, cols)

        @pl.when(c != d % 2)
        def _():
            core_out[f, h] = grad.astype(BF16).reshape(4, 4, half, cols)
            core_copy(f, h).start()

        return carry

    lax.fori_loop(0, 8, backward, 0)
    for h in range(2):
        span = slice(cols * h, cols * h + cols)
        ig_ref[:, span] = (m[n, h].astype(F32) + igacc[:, span]).astype(BF16)

    for f in range(2):
        for h in range(2):
            core_copy(f, h).wait_recv()
            gk[f, h] += core_in[f, h].astype(F32)

    ring1, ring2 = [], []
    for f in range(2):
        first = (x_next, x_prev) if f == 0 else (y_next, y_prev)
        second = (y_next, y_prev) if f == 0 else (x_next, x_prev)
        ring1.append(
            Ring(copy, WIDE_RS + 6 * f, w_out.at[f], w_opp.at[f], w_left.at[f], w_right.at[f], *first)
        )
        ring2.append(
            Ring(copy, WIDE_RS + 12 + 6 * f, v_out.at[f], v_opp.at[f], v_left.at[f], v_right.at[f], *second)
        )

    def outer(f, da):
        if f == 0:
            return lambda h: gk[0, h, :, (x + da) % 4]
        return lambda h: gk[1, h, (y + da) % 4]

    def inner(f, db):
        mine = y if f == 0 else x
        return lambda h: hk[f, h, (mine + db) % 4]

    for rings, load in ((ring1, outer), (ring2, inner)):
        for f in range(2):
            rings[f].send_far(load(f, 2))
        for f in range(2):
            rings[f].send_right_early(load(f, 1))
            rings[f].send_left_early(load(f, 3))
        for f in range(2):
            rings[f].send_right_late(load(f, 1))
            rings[f].send_left_late(load(f, 3))
        for f in range(2):
            for h in range(2):
                rings[f].wait_half(h)
                total = load(f, 0)(h) + rings[f].received(h)
                if rings is ring1:
                    hk[f, h] = total
                else:
                    res[f, h] = total

    z_out[...] = res[1 - zl].astype(BF16)
    z_sum = copy(z_out, z_in, ZSUM, z_other)
    z_sum.start()
    z_sum.wait_recv()
    scale = 1.0 / (tokens * 64.0) ** 0.5
    for h in range(2):
        fin[:, cols * h : cols * h + cols] = (res[zl, h] + z_in[h].astype(F32)) * scale
    final = copy(fin, wg_ref, FINAL, target_id)

    @pl.when(own_piece)
    def _():
        local = pltpu.make_async_copy(fin, wg_ref, local_sem)
        local.start()
        local.wait()

    @pl.when(jnp.logical_not(own_piece))
    def _():
        final.start()
        final.wait_recv()
        final.wait_send()

    z_sum.wait_send()
    for item in sent + sq_copies + ag:
        item.wait_send()
    sibling_all.wait_send()
    ring.wait_sends()
    for one in ring1 + ring2:
        one.wait_sends()
    for f in range(2):
        for h in range(2):
            core_copy(f, h).wait_send()

    @pl.when(n == owner)
    def _():
        for item in w_copies:
            item.wait_send()


def shards(teacher_rows, teacher_gain, projector, student_rows, student_weight):
    tokens, kt = teacher_rows.shape
    ks = student_rows.shape[1]
    width = projector.shape[1]
    half, cols, depth = width // 2, ks // 2, kt + ks
    c, w = lax.axis_index("section"), lax.axis_index("wide")
    weight_cols = lax.dynamic_slice(student_weight, (0, width * (w % 8) + half * c), (4 * ks, half))
    weight_t = weight_cols.reshape(4, ks, half).transpose(0, 2, 1)
    vmem = pl.BlockSpec(memory_space=pltpu.VMEM)
    return pl.pallas_call(
        kernel,
        out_shape=(
            jax.ShapeDtypeStruct((tokens, ks), BF16),
            jax.ShapeDtypeStruct((half, ks), F32),
        ),
        in_specs=[vmem] * 6,
        out_specs=(vmem, vmem),
        scratch_shapes=[
            pltpu.VMEM((32, width, depth), BF16),
            pltpu.VMEM((tokens, depth), BF16),
            pltpu.VMEM((tokens, kt), BF16),
            pltpu.VMEM((4, 8, 128), F32),
            pltpu.VMEM((4, 2, tokens, cols), F32),
            pltpu.VMEM((3, 2, tokens, cols), BF16),
            pltpu.VMEM((2, tokens, cols), BF16),
            pltpu.VMEM((2, tokens, cols), BF16),
            pltpu.VMEM((2, tokens, cols), BF16),
            pltpu.VMEM((4, 2, tokens, cols), BF16),
            pltpu.VMEM((tokens, ks), F32),
            pltpu.VMEM((2, 2, 4, 4, half, cols), F32),
            pltpu.VMEM((2, 2, 4, 4, half, cols), BF16),
            pltpu.VMEM((2, 2, 4, 4, half, cols), BF16),
            pltpu.VMEM((2, 3, 2, 4, half, cols), BF16),
            pltpu.VMEM((2, 2, 4, half, cols), BF16),
            pltpu.VMEM((2, 2, 4, half, cols), BF16),
            pltpu.VMEM((2, 2, 4, half, cols), BF16),
            pltpu.VMEM((2, 2, 4, half, cols), F32),
            pltpu.VMEM((2, 3, 2, half, cols), BF16),
            pltpu.VMEM((2, 2, half, cols), BF16),
            pltpu.VMEM((2, 2, half, cols), BF16),
            pltpu.VMEM((2, 2, half, cols), BF16),
            pltpu.VMEM((2, 2, half, cols), F32),
            pltpu.VMEM((2, half, cols), BF16),
            pltpu.VMEM((2, half, cols), BF16),
            pltpu.VMEM((half, ks), F32),
            pltpu.SemaphoreType.DMA((SLOTS,)),
            pltpu.SemaphoreType.DMA((SLOTS,)),
            pltpu.SemaphoreType.DMA,
        ],
        compiler_params=pltpu.CompilerParams(
            collective_id=0, has_side_effects=True, vmem_limit_bytes=60 * 2**20
        ),
    )(
        teacher_rows,
        teacher_gain.reshape(1, kt),
        projector.T,
        weight_t,
        student_rows,
        student_rows.T,
    )


def solution(mesh):
    placed = (
        P(("section", "wide"), "narrow"),
        P("narrow"),
        P("narrow", "wide"),
        P(("section", "wide"), "narrow"),
        P(None, "narrow"),
    )
    return jax.shard_map(
        shards,
        mesh=mesh,
        in_specs=placed,
        out_specs=(P(("section", "wide"), "narrow"), P(("section", "wide"), "narrow")),
        check_vma=False,
    )
```

time: 701 us -> 192 us (0.27)
  the two profiles are of different devices: /device:TPU:32 before, /device:TPU:1 now
where the time goes in v1:
time: 192 us
  Pallas kernels  182 us (95%)
  local copies, waits for them, and re-layouts  9.6 us (5%)
    pallas_call x1, Pallas kernels, shards(): pl.pallas_call(kernel, out_shape=(jax.ShapeDtypeStruct((tokens, ks), BF16...  182 us
    unnamed x3, local copies, waits for them, and re-layouts  5.61 us

profile of v1, /device:TPU:1, one launch (start us, length us, event | category | flops | bytes accessed | tf_op | source)
XLA Modules:
  0.0 192.0 jit_solution(15412950036495388379)
XLA Ops:
  0.6 1.7 constant_dynamic-slice_fusion
  2.4 1.0 copy.9
  3.4 2.1 %copy.10 = bf16[384,768]{0,1:T(8,128)(2,1)} copy(bf16[384,768]{1,0:T(8,128)(2,1)} %x_ref.1) | data formatting | bytes 1179648 | tf_op args[3]
  5.5 1.3 reshape.10.g_ref
  6.8 181.8 %shard_map.68 = (bf16[384,768]{1,0:T(8,128)(2,1)}, f32[48,768]{1,0:T(8,128)}) custom-call(bf16[384,1664]{1,0:T(8,128)(2,1)} %t_ref.1, bf16[1,1664]{1,0:T(2,128)(2,1)} %reshape.10.g_ref, bf16[96,1664]{1,0:T(8,128)(2,1)} %bitcast.7, bf16[4,48,768]{2,1,0:T(8,128)(2,1)} %bitcast.6, bf16[384,768]{1,0:T(8,128)(2,1)} %x_ref.1, bf16[768,384]{1,0:T(8,128)(2,1)} %bitcast.5), custom_call_target="tpu_custom_call" | custom-call | tf_op jit(solution)/shard_map/pallas_call | solution.py:458
  188.5 1.9 copy.15
  190.4 1.6 copy.16

commit v2 on v0

v2 whole, which is shorter than its diff:
```python
import functools

import jax
import jax.numpy as jnp
from jax import lax
from jax.experimental import pallas as pl
from jax.experimental.pallas import tpu as pltpu
from jax.sharding import PartitionSpec as P

MESH = pl.DeviceIdType.MESH
F32 = jnp.float32
BF16 = jnp.bfloat16

GATHER = 0
ZSWAP = 40
WSEND = 41
WRECV = 44
SQUARES = 45
PAIRED = 48
SIBLING = 49
NARROW_RS = 51
NARROW_AG = 57
CORE_SUM = 63
WIDE_RS = 67
FINAL = 71
SLOTS = 75


def kernel(
    t_ref, g_ref, pt_ref, wt_ref, x_ref, xt_ref, ig_ref, wg_ref,
    ct, lhs, hid, sq, part, far_out, near_out, far_in, near_in, m, igacc,
    kept, core_out, core_in, wide_out, wide_in, fin_out, fin_in, send_sem, recv_sem,
):
    c = lax.axis_index("section")
    w = lax.axis_index("wide")
    n = lax.axis_index("narrow")
    x, y, zl = w % 4, (w // 4) % 4, w // 16
    tokens, kt = t_ref.shape
    ks = x_ref.shape[1]
    half = pt_ref.shape[0] // 2
    depth = kt + ks
    cut = (depth // 256 + 1) * 128
    cols = ks // 2
    rows = pl.ds(pl.multiple_of(half * c, half), half)

    def at(zz, yy, xx):
        return zz * 16 + yy * 4 + xx

    sibling = {"section": 1 - c}
    z_other = {"wide": at(1 - zl, y, x)}
    n_dev = [None] + [{"narrow": (n + d) % 4} for d in (1, 2, 3)]

    def peer(k):
        return (y + k // 4) % 4, (x + k % 4) % 4

    def target(d):
        return {"section": n // 2, "wide": at(n % 2, y, x), "narrow": (n + d) % 4}

    at_home = n == 2 * c + zl
    sources = [
        ({"section": cc, "wide": at(zz, y, x), "narrow": 2 * c + zl}, jnp.logical_and(at_home, jnp.logical_and(cc == c, zz == zl)))
        for zz in range(2)
        for cc in range(2)
    ]

    barrier = pltpu.get_barrier_semaphore()
    greeted = [sibling, z_other, n_dev[1], n_dev[2], n_dev[3]]
    for device in greeted:
        pl.semaphore_signal(barrier, inc=1, device_id=device, device_id_type=MESH)

    def greet(k, carry):
        yy, xx = peer(k)
        pl.semaphore_signal(barrier, inc=1, device_id={"wide": at(zl, yy, xx)}, device_id_type=MESH)
        return carry

    lax.fori_loop(1, 16, greet, 0)
    for device, mine in sources:

        @pl.when(jnp.logical_not(mine))
        def _():
            pl.semaphore_signal(barrier, inc=1, device_id=device, device_id_type=MESH)

    pl.semaphore_wait(barrier, jnp.where(at_home, len(greeted) + 18, len(greeted) + 19))

    def copy(src, dst, slot, device):
        return pltpu.make_async_remote_copy(
            src_ref=src, dst_ref=dst, send_sem=send_sem.at[slot], recv_sem=recv_sem.at[slot],
            device_id=device, device_id_type=MESH,
        )

    w_cols = pl.ds(kt, ks)
    w_home = ct.at[w, rows, w_cols]
    owner = w // 8
    w_copies = [
        pltpu.make_async_remote_copy(
            src_ref=wt_ref.at[(n + d) % 4], dst_ref=w_home, send_sem=send_sem.at[WSEND + d - 1],
            recv_sem=recv_sem.at[WRECV], device_id=n_dev[d], device_id_type=MESH,
        )
        for d in (1, 2, 3)
    ]

    @pl.when(n == owner)
    def _():
        for item in w_copies:
            item.start()
        ct[w, rows, w_cols] = wt_ref[n]

    ct[w, rows, pl.ds(0, kt)] = pt_ref[rows, :]

    eye = lax.broadcasted_iota(jnp.int32, (128, 128), 0) == lax.broadcasted_iota(jnp.int32, (128, 128), 1)
    groups = tokens // 128
    sq[0] = jnp.zeros((8, 128), F32)
    for i in range(groups):
        part_t = t_ref[128 * i : 128 * i + 128, :].astype(F32)
        col = jnp.sum(part_t * part_t, axis=1, keepdims=True)
        sq[0, i : i + 1, :] = jnp.sum(jnp.where(eye, col, 0.0), axis=0, keepdims=True)
    sq_copies = [copy(sq.at[0], sq.at[d], SQUARES + d - 1, n_dev[d]) for d in (1, 2, 3)]
    for item in sq_copies:
        item.start()

    @pl.when(n != owner)
    def _():
        w_copies[0].wait_recv()

    def slab(index, part=None):
        if part is None:
            return ct.at[index, rows]
        return ct.at[index, rows, pl.ds(0, cut) if part == 0 else pl.ds(cut, depth - cut)]

    def spread(index, slot, device, part=None):
        return copy(slab(index, part), slab(index, part), slot, device)

    sent = []

    def go(item):
        item.start()
        sent.append(item)

    along_a, along_b = jnp.where(c == 0, x, y), jnp.where(c == 0, y, x)

    def cell(plane, da, db):
        a, b = (along_a + da) % 4, (along_b + db) % 4
        return plane * 16 + jnp.where(c == 0, 4 * b + a, 4 * a + b)

    first = [{"wide": cell(zl, 1, 0)}, {"wide": cell(zl, 3, 0)}]
    second = [{"wide": cell(zl, 0, 1)}, {"wide": cell(zl, 0, 3)}]
    ALONG = (0, 3, 1, 2)

    class Plane:
        def __init__(self, p, plane):
            self.base, self.p, self.plane = GATHER + 20 * p, p, plane

        def to_sibling(self, index):
            copy(slab(index), slab(index), SIBLING + self.p, sibling).start()

        def whole(self):
            planes = ct.at[pl.ds(16 * self.plane, 16), rows]
            return copy(planes, planes, SIBLING + self.p, sibling)

        def begin(self):
            own = cell(self.plane, 0, 0)
            for side in range(2):
                go(spread(own, self.base + side, first[side]))
            self.second_send(0)
            self.to_sibling(own)

        def second_send(self, j):
            index = cell(self.plane, ALONG[j], 0)
            for side in range(2):
                go(spread(index, self.base + 4 + 4 * j + side, second[side]))

        def first_near(self):
            for side in range(2):
                index = cell(self.plane, ALONG[1 + side], 0)
                spread(index, self.base + side, first[side]).wait_recv()
                go(spread(index, self.base + 2 + side, first[side], side))
                self.second_send(1 + side)
                self.to_sibling(index)

        def first_far(self):
            index = cell(self.plane, 2, 0)
            for side in range(2):
                spread(index, self.base + 2 + side, first[side], side).wait_recv()
            self.second_send(3)
            self.to_sibling(index)

        def second_near(self, j):
            slot = self.base + 4 + 4 * j
            for side in range(2):
                index = cell(self.plane, ALONG[j], 3 if side == 0 else 1)
                spread(index, slot + side, second[side]).wait_recv()
                go(spread(index, slot + 2 + side, second[side], side))
                self.to_sibling(index)

        def second_far(self, j):
            slot = self.base + 4 + 4 * j
            index = cell(self.plane, ALONG[j], 2)
            for side in range(2):
                spread(index, slot + 2 + side, second[side], side).wait_recv()
            self.to_sibling(index)

    p_first = 1 - n // 2
    near_plane, far_plane = Plane(0, p_first), Plane(1, 1 - p_first)
    z_copy = spread(w, ZSWAP, z_other)
    go(z_copy)

    @pl.when(zl != p_first)
    def _():
        z_copy.wait_recv()

    near_plane.begin()

    lhs[:, kt:] = x_ref[...]
    for item in sq_copies:
        item.wait_recv()
    inverse = lax.rsqrt((sq[0] + sq[1] + sq[2] + sq[3]) / (4 * kt) + 1e-05)
    gain = g_ref[...].astype(F32)
    for i in range(groups):
        col = jnp.sum(jnp.where(eye, inverse[i : i + 1, :], 0.0), axis=1, keepdims=True)
        span = slice(128 * i, 128 * i + 128)
        hid[span, :] = -(t_ref[span, :].astype(F32) * col * gain).astype(BF16)
    paired_copy = copy(hid, lhs.at[:, pl.ds(0, kt)], PAIRED, sibling)
    go(paired_copy)

    near_plane.first_near()
    near_plane.second_near(0)
    near_plane.first_far()
    near_plane.second_near(1)
    near_plane.second_far(0)
    near_plane.second_near(2)
    near_plane.second_far(1)
    near_plane.second_near(3)

    @pl.when(zl == p_first)
    def _():
        z_copy.wait_recv()

    far_plane.begin()
    near_plane.second_far(2)
    near_plane.second_far(3)
    paired_copy.wait_recv()
    near_plane.whole().wait_recv()

    e2 = n % 2
    e1 = 1 - e2

    def by(e):
        return {"narrow": (n + 1 + 2 * e) % 4}

    def far_copy(e):
        return copy(far_out.at[e], far_in.at[e], NARROW_RS + e, by(e))

    def early_copy(e):
        return copy(near_out.at[e, 1 - e], near_in.at[e, 1 - e], NARROW_RS + 2 + e, by(e))

    def late_copy(e):
        return copy(near_out.at[e, e], near_in.at[e, e], NARROW_RS + 4 + e, by(e))

    def product(b, h):
        block = ct[pl.ds(8 * b + 4 * h, 4)].reshape(cols, depth)
        return lax.dot_general(lhs[...], block, (((1,), (1,)), ((), ())), preferred_element_type=F32)

    def far_block(e, carry):
        far_out[e] = product((n + 2) % 4, e).astype(BF16)
        far_copy(e).start()
        return carry

    def near_block(e):
        def step(k, carry):
            h = jnp.where(k == 0, 1 - e, e)
            part[h] = product((n + 1 + 2 * e) % 4, h)

            @pl.when(k == 0)
            def _():
                near_out[e, h] = part[h].astype(BF16)
                early_copy(e).start()

            return carry

        lax.fori_loop(0, 2, step, 0)

    def send_late(e):
        far_copy(e).wait_recv()
        near_out[e, e] = (part[e] + far_in[e].astype(F32)).astype(BF16)
        late_copy(e).start()

    lax.fori_loop(0, 2, far_block, 0)
    far_plane.first_near()
    near_block(e1)
    far_plane.second_near(0)
    far_plane.first_far()
    far_plane.second_near(1)
    far_plane.second_far(0)
    far_plane.second_near(2)
    far_plane.second_far(1)
    far_plane.second_near(3)
    send_late(e1)
    far_plane.second_far(2)
    far_plane.second_far(3)
    far_plane.whole().wait_recv()
    near_block(e2)
    send_late(e2)

    def own_block(h, carry):
        span = pl.ds(pl.multiple_of(cols * h, cols), cols)
        part[h] = product(n, h) + x_ref[:, span].astype(F32)
        return carry

    lax.fori_loop(0, 2, own_block, 0)

    def ag(block, h, e, slot):
        return copy(m.at[block, h], m.at[block, h], NARROW_AG + slot, by(e))

    def own_copy(h, e):
        return ag(n, h, e, 2 * e + h)

    def pass_on(e):
        return ag((n + 3 + 2 * e) % 4, e, e, 4 + e)

    early_copy(e2).wait_recv()
    late_copy(e2).wait_recv()

    def finish(k, carry):
        h = jnp.where(k == 0, 1 - e1, e1)

        @pl.when(k == 0)
        def _():
            early_copy(e1).wait_recv()

        @pl.when(k == 1)
        def _():
            late_copy(e1).wait_recv()

        m[n, h] = (part[h] + near_in[0, h].astype(F32) + near_in[1, h].astype(F32)).astype(BF16)
        own_copy(h, 0).start()
        own_copy(h, 1).start()
        return carry

    lax.fori_loop(0, 2, finish, 0)
    igacc[...] = jnp.zeros((tokens, ks), F32)

    def core_copy(d):
        return copy(core_out.at[d], core_in.at[d], CORE_SUM + d, sibling)

    me = 4 * y + x

    def wide_send(d):
        def one(k, carry):
            yy, xx = peer(k)
            copy(
                wide_out.at[d, 4 * yy + xx], wide_in.at[d, me], WIDE_RS + d, {"wide": at(zl, yy, xx)}
            ).start()
            return carry

        lax.fori_loop(1, 16, one, 0)

    def wide_all(d):
        return copy(
            wide_out.at[d, pl.ds(0, 15)], wide_in.at[d, pl.ds(0, 15)], WIDE_RS + d, {"wide": at(zl, y, (x + 1) % 4)}
        )

    def final_copy(d):
        return pltpu.make_async_remote_copy(
            src_ref=fin_out.at[d], dst_ref=fin_in.at[zl, c], send_sem=send_sem.at[FINAL + d],
            recv_sem=recv_sem.at[FINAL + 2 * zl + c], device_id=target(d), device_id_type=MESH,
        )

    def reduce(d):
        wide_all(d).wait_recv()
        total = wide_in[d, 0].astype(F32)
        for k in range(1, 16):
            total = total + wide_in[d, k].astype(F32)
        stays = jnp.logical_and(at_home, d == 0)

        @pl.when(stays)
        def _():
            fin_in[zl, c] = total.astype(BF16)

        @pl.when(jnp.logical_not(stays))
        def _():
            fin_out[d] = total.astype(BF16)
            final_copy(d).start()

    def order(r):
        return jnp.where(r == 0, 0, jnp.where(r == 1, 3, jnp.where(r == 2, 1, 2)))

    def backward(i, carry):
        r = i // 2

        @pl.when(i == 2)
        def _():
            own_copy(0, 0).wait_recv()
            pass_on(0).start()
            own_copy(1, 1).wait_recv()
            pass_on(1).start()
            own_copy(1, 0).wait_recv()

        @pl.when(i == 4)
        def _():
            own_copy(0, 1).wait_recv()

        @pl.when(i == 6)
        def _():
            reduce(0)
            pass_on(0).wait_recv()
            pass_on(1).wait_recv()

        d = order(r)
        h = jnp.where(i % 2 == 0, 1 - c, c)
        b = (n + d) % 4
        piece = m[b, h]
        block = ct[pl.ds(8 * b + 4 * h, 4), :, pl.ds(kt, ks)].reshape(cols, ks)
        grad = jnp.dot(xt_ref[...], piece, preferred_element_type=F32)

        @pl.when(i % 2 == 0)
        def _():
            core_out[d] = grad.astype(BF16)
            core_copy(d).start()

        @pl.when(i % 2 == 1)
        def _():
            kept[...] = grad

        igacc[...] += jnp.dot(piece, block, preferred_element_type=F32)

        @pl.when(i % 2 == 1)
        def _():
            core_copy(d).wait_recv()
            both = (kept[...] + core_in[d].astype(F32)).astype(BF16).reshape(16, half, cols)
            wide_out[d] = both
            wide_in[d, me] = wide_out[d, me]
            wide_send(d)

        return carry

    lax.fori_loop(0, 8, backward, 0)
    for h in range(2):
        span = slice(cols * h, cols * h + cols)
        ig_ref[:, span] = (m[n, h].astype(F32) + igacc[:, span]).astype(BF16)

    def reduce_rest(r, carry):
        reduce(order(r))
        return carry

    lax.fori_loop(1, 4, reduce_rest, 0)
    scale = 1.0 / (tokens * 64.0) ** 0.5
    for zz in range(2):
        for cc in range(2):

            @pl.when(jnp.logical_not(sources[2 * zz + cc][1]))
            def _():
                pltpu.make_async_remote_copy(
                    src_ref=fin_out.at[0], dst_ref=fin_in.at[zz, cc], send_sem=send_sem.at[FINAL],
                    recv_sem=recv_sem.at[FINAL + 2 * zz + cc], device_id=sibling, device_id_type=MESH,
                ).wait_recv()

    for h in range(2):
        wg_ref[:, cols * h : cols * h + cols] = (fin_in[0, h].astype(F32) + fin_in[1, h].astype(F32)) * scale

    for item in sent + sq_copies:
        item.wait_send()
    near_plane.whole().wait_send()
    far_plane.whole().wait_send()
    for e in range(2):
        far_copy(e).wait_send()
        early_copy(e).wait_send()
        late_copy(e).wait_send()
        pass_on(e).wait_send()
        for h in range(2):
            own_copy(h, e).wait_send()
    for d in range(4):
        core_copy(d).wait_send()
        wide_all(d).wait_send()

        @pl.when(jnp.logical_not(jnp.logical_and(at_home, d == 0)))
        def _():
            final_copy(d).wait_send()

    @pl.when(n == owner)
    def _():
        for item in w_copies:
            item.wait_send()


def shards(teacher_rows, teacher_gain, projector, student_rows, student_weight):
    tokens, kt = teacher_rows.shape
    ks = student_rows.shape[1]
    width = projector.shape[1]
    half, cols, depth = width // 2, ks // 2, kt + ks
    c, w = lax.axis_index("section"), lax.axis_index("wide")
    weight_cols = lax.dynamic_slice(student_weight, (0, width * (w % 8) + half * c), (4 * ks, half))
    weight_t = weight_cols.reshape(4, ks, half).transpose(0, 2, 1)
    vmem = pl.BlockSpec(memory_space=pltpu.VMEM)
    return pl.pallas_call(
        kernel,
        out_shape=(
            jax.ShapeDtypeStruct((tokens, ks), BF16),
            jax.ShapeDtypeStruct((half, ks), F32),
        ),
        in_specs=[vmem] * 6,
        out_specs=(vmem, vmem),
        scratch_shapes=[
            pltpu.VMEM((32, width, depth), BF16),
            pltpu.VMEM((tokens, depth), BF16),
            pltpu.VMEM((tokens, kt), BF16),
            pltpu.VMEM((4, 8, 128), F32),
            pltpu.VMEM((2, tokens, cols), F32),
            pltpu.VMEM((2, tokens, cols), BF16),
            pltpu.VMEM((2, 2, tokens, cols), BF16),
            pltpu.VMEM((2, tokens, cols), BF16),
            pltpu.VMEM((2, 2, tokens, cols), BF16),
            pltpu.VMEM((4, 2, tokens, cols), BF16),
            pltpu.VMEM((tokens, ks), F32),
            pltpu.VMEM((ks, cols), F32),
            pltpu.VMEM((4, ks, cols), BF16),
            pltpu.VMEM((4, ks, cols), BF16),
            pltpu.VMEM((4, 16, half, cols), BF16),
            pltpu.VMEM((4, 16, half, cols), BF16),
            pltpu.VMEM((4, half, cols), BF16),
            pltpu.VMEM((2, 2, half, cols), BF16),
            pltpu.SemaphoreType.DMA((SLOTS,)),
            pltpu.SemaphoreType.DMA((SLOTS,)),
        ],
        compiler_params=pltpu.CompilerParams(
            collective_id=0, has_side_effects=True, vmem_limit_bytes=60 * 2**20
        ),
    )(
        teacher_rows,
        teacher_gain.reshape(1, kt),
        projector.T,
        weight_t,
        student_rows,
        student_rows.T,
    )


def solution(mesh):
    placed = (
        P(("section", "wide"), "narrow"),
        P("narrow"),
        P("narrow", "wide"),
        P(("section", "wide"), "narrow"),
        P(None, "narrow"),
    )
    return jax.shard_map(
        shards,
        mesh=mesh,
        in_specs=placed,
        out_specs=(P(("section", "wide"), "narrow"), P(("section", "wide"), "narrow")),
        check_vma=False,
    )
```

time: 701 us -> 179 us (0.26)
  the two profiles are of different devices: /device:TPU:32 before, /device:TPU:1 now
where the time goes in v2:
time: 179 us; the launch traced here: 175 us
  Pallas kernels  165 us (92%)
  local copies, waits for them, and re-layouts  9.6 us (5%)
    pallas_call x1, Pallas kernels, shards(): pl.pallas_call(kernel, out_shape=(jax.ShapeDtypeStruct((tokens, ks), BF16...  165 us
    unnamed x3, local copies, waits for them, and re-layouts  5.61 us

profile of v2, /device:TPU:1, one launch (start us, length us, event | category | flops | bytes accessed | tf_op | source)
XLA Modules:
  0.0 175.5 jit_solution(8399518421034799055)
XLA Ops:
  0.6 1.7 constant_dynamic-slice_fusion
  2.4 1.0 copy.9
  3.4 2.1 %copy.10 = bf16[384,768]{0,1:T(8,128)(2,1)} copy(bf16[384,768]{1,0:T(8,128)(2,1)} %x_ref.1) | data formatting | bytes 1179648 | tf_op args[3]
  5.5 1.3 reshape.10.g_ref
  6.8 165.2 %shard_map.68 = (bf16[384,768]{1,0:T(8,128)(2,1)}, f32[48,768]{1,0:T(8,128)}) custom-call(bf16[384,1664]{1,0:T(8,128)(2,1)} %t_ref.1, bf16[1,1664]{1,0:T(2,128)(2,1)} %reshape.10.g_ref, bf16[96,1664]{1,0:T(8,128)(2,1)} %bitcast.7, bf16[4,48,768]{2,1,0:T(8,128)(2,1)} %bitcast.6, bf16[384,768]{1,0:T(8,128)(2,1)} %x_ref.1, bf16[768,384]{1,0:T(8,128)(2,1)} %bitcast.5), custom_call_target="tpu_custom_call" | custom-call | tf_op jit(solution)/shard_map/pallas_call | solution.py:494
  172.0 1.9 %copy.15 = bf16[384,768]{1,0:T(8,128)(2,1)} copy(bf16[384,768]{1,0:T(8,128)(2,1)} %get-tuple-element.4) | data formatting | bytes 1179648
  173.9 1.6 copy.16

commit v3 on v2

--- a/solution.py
+++ b/solution.py
@@ -13,23 +13,22 @@
 
 GATHER = 0
 ZSWAP = 40
-WSEND = 41
-WRECV = 44
-SQUARES = 45
-PAIRED = 48
-SIBLING = 49
-NARROW_RS = 51
-NARROW_AG = 57
-CORE_SUM = 63
-WIDE_RS = 67
-FINAL = 71
-SLOTS = 75
+WEIGHT = 41
+SQUARES = 49
+PAIRED = 52
+SIBLING = 53
+NARROW_RS = 55
+NARROW_AG = 61
+CORE_SUM = 67
+WIDE_RS = 71
+FINAL = 75
+SLOTS = 79
 
 
 def kernel(
-    t_ref, g_ref, pt_ref, wt_ref, x_ref, xt_ref, ig_ref, wg_ref,
+    t_ref, g_ref, pt_ref, x_ref, weight_ref, ig_ref, wg_ref, window, wt_ref, xt_ref,
     ct, lhs, hid, sq, part, far_out, near_out, far_in, near_in, m, igacc,
-    kept, core_out, core_in, wide_out, wide_in, fin_out, fin_in, send_sem, recv_sem,
+    kept, core_out, core_in, wide_out, wide_in, fin_out, fin_in, send_sem, recv_sem, local_sem,
 ):
     c = lax.axis_index("section")
     w = lax.axis_index("wide")
@@ -63,8 +62,18 @@
         for cc in range(2)
     ]
 
+    owner = w // 8
+    column = 2 * half * (w % 8) + half * c
+    low = jnp.minimum(column // 128 * 128, ks - 256)
+    fetch = pltpu.make_async_copy(weight_ref.at[:, pl.ds(pl.multiple_of(low, 128), 256)], window, local_sem)
+
+    @pl.when(n == owner)
+    def _():
+        fetch.start()
+
     barrier = pltpu.get_barrier_semaphore()
-    greeted = [sibling, z_other, n_dev[1], n_dev[2], n_dev[3]]
+    z_dev = [{"wide": at(1 - zl, y, x), "narrow": (n + d) % 4} for d in range(4)]
+    greeted = [sibling, n_dev[1], n_dev[2], n_dev[3]] + z_dev
     for device in greeted:
         pl.semaphore_signal(barrier, inc=1, device_id=device, device_id_type=MESH)
 
@@ -88,24 +97,33 @@
             device_id=device, device_id_type=MESH,
         )
 
-    w_cols = pl.ds(kt, ks)
-    w_home = ct.at[w, rows, w_cols]
-    owner = w // 8
-    w_copies = [
-        pltpu.make_async_remote_copy(
-            src_ref=wt_ref.at[(n + d) % 4], dst_ref=w_home, send_sem=send_sem.at[WSEND + d - 1],
-            recv_sem=recv_sem.at[WRECV], device_id=n_dev[d], device_id_type=MESH,
+    w_cols, p_cols = pl.ds(kt, ks), pl.ds(0, kt)
+
+    def weight_copy(k):
+        return pltpu.make_async_remote_copy(
+            src_ref=wt_ref.at[(n + k) % 4], dst_ref=ct.at[w, rows, w_cols], send_sem=send_sem.at[WEIGHT + k],
+            recv_sem=recv_sem.at[WEIGHT + k // 4], device_id=(n_dev[k] if k < 4 else z_dev[k - 4]),
+            device_id_type=MESH,
         )
-        for d in (1, 2, 3)
-    ]
+
+    w_other = at(1 - zl, y, x)
+    ct[w, rows, p_cols] = pt_ref[rows, :]
+    z_copy = copy(ct.at[w, rows, p_cols], ct.at[w, rows, p_cols], ZSWAP, z_other)
+    z_copy.start()
 
     @pl.when(n == owner)
     def _():
-        for item in w_copies:
-            item.start()
+        fetch.wait()
+        row = lax.broadcasted_iota(jnp.int32, (half, 256), 0)
+        lane = lax.broadcasted_iota(jnp.int32, (half, 256), 1)
+        pick = jnp.where(lane == row + (column - low), 1.0, 0.0).astype(BF16)
+        for q in range(4):
+            wt_ref[q] = lax.dot_general(
+                pick, window[ks * q : ks * q + ks, :], (((1,), (1,)), ((), ())), preferred_element_type=F32
+            ).astype(BF16)
+        for k in (1, 5, 2, 6, 3, 7, 4):
+            weight_copy(k).start()
         ct[w, rows, w_cols] = wt_ref[n]
-
-    ct[w, rows, pl.ds(0, kt)] = pt_ref[rows, :]
 
     eye = lax.broadcasted_iota(jnp.int32, (128, 128), 0) == lax.broadcasted_iota(jnp.int32, (128, 128), 1)
     groups = tokens // 128
@@ -118,9 +136,15 @@
     for item in sq_copies:
         item.start()
 
-    @pl.when(n != owner)
-    def _():
-        w_copies[0].wait_recv()
+    def weight_arrives(plane):
+        @pl.when(jnp.logical_and(zl == plane, n != owner))
+        def _():
+            weight_copy(1).wait_recv()
+
+        @pl.when(zl != plane)
+        def _():
+            weight_copy(5).wait_recv()
+            z_copy.wait_recv()
 
     def slab(index, part=None):
         if part is None:
@@ -142,7 +166,7 @@
         a, b = (along_a + da) % 4, (along_b + db) % 4
         return plane * 16 + jnp.where(c == 0, 4 * b + a, 4 * a + b)
 
-    first = [{"wide": cell(zl, 1, 0)}, {"wide": cell(zl, 3, 0)}]
+    first = [{"wide": cell(zl, 1, 0)}, {"wide": cell(zl, 3, 0)}, {"wide": cell(zl, 2, 0)}]
     second = [{"wide": cell(zl, 0, 1)}, {"wide": cell(zl, 0, 3)}]
     ALONG = (0, 3, 1, 2)
 
@@ -158,8 +182,9 @@
             return copy(planes, planes, SIBLING + self.p, sibling)
 
         def begin(self):
+            weight_arrives(self.plane)
             own = cell(self.plane, 0, 0)
-            for side in range(2):
+            for side in range(3):
                 go(spread(own, self.base + side, first[side]))
             self.second_send(0)
             self.to_sibling(own)
@@ -173,14 +198,12 @@
             for side in range(2):
                 index = cell(self.plane, ALONG[1 + side], 0)
                 spread(index, self.base + side, first[side]).wait_recv()
-                go(spread(index, self.base + 2 + side, first[side], side))
                 self.second_send(1 + side)
                 self.to_sibling(index)
 
         def first_far(self):
             index = cell(self.plane, 2, 0)
-            for side in range(2):
-                spread(index, self.base + 2 + side, first[side], side).wait_recv()
+            spread(index, self.base + 2, first[2]).wait_recv()
             self.second_send(3)
             self.to_sibling(index)
 
@@ -201,20 +224,14 @@
 
     p_first = 1 - n // 2
     near_plane, far_plane = Plane(0, p_first), Plane(1, 1 - p_first)
-    z_copy = spread(w, ZSWAP, z_other)
-    go(z_copy)
-
-    @pl.when(zl != p_first)
-    def _():
-        z_copy.wait_recv()
-
     near_plane.begin()
 
     lhs[:, kt:] = x_ref[...]
+    xt_ref[...] = x_ref[...].T
     for item in sq_copies:
         item.wait_recv()
     inverse = lax.rsqrt((sq[0] + sq[1] + sq[2] + sq[3]) / (4 * kt) + 1e-05)
-    gain = g_ref[...].astype(F32)
+    gain = g_ref[...].astype(F32).reshape(1, kt)
     for i in range(groups):
         col = jnp.sum(jnp.where(eye, inverse[i : i + 1, :], 0.0), axis=1, keepdims=True)
         span = slice(128 * i, 128 * i + 128)
@@ -229,13 +246,8 @@
     near_plane.second_far(0)
     near_plane.second_near(2)
     near_plane.second_far(1)
+    far_plane.begin()
     near_plane.second_near(3)
-
-    @pl.when(zl == p_first)
-    def _():
-        z_copy.wait_recv()
-
-    far_plane.begin()
     near_plane.second_far(2)
     near_plane.second_far(3)
     paired_copy.wait_recv()
@@ -457,7 +469,7 @@
     for h in range(2):
         wg_ref[:, cols * h : cols * h + cols] = (fin_in[0, h].astype(F32) + fin_in[1, h].astype(F32)) * scale
 
-    for item in sent + sq_copies:
+    for item in sent + sq_copies + [z_copy]:
         item.wait_send()
     near_plane.whole().wait_send()
     far_plane.whole().wait_send()
@@ -478,8 +490,8 @@
 
     @pl.when(n == owner)
     def _():
-        for item in w_copies:
-            item.wait_send()
+        for k in range(1, 8):
+            weight_copy(k).wait_send()
 
 
 def shards(teacher_rows, teacher_gain, projector, student_rows, student_weight):
@@ -487,9 +499,6 @@
     ks = student_rows.shape[1]
     width = projector.shape[1]
     half, cols, depth = width // 2, ks // 2, kt + ks
-    c, w = lax.axis_index("section"), lax.axis_index("wide")
-    weight_cols = lax.dynamic_slice(student_weight, (0, width * (w % 8) + half * c), (4 * ks, half))
-    weight_t = weight_cols.reshape(4, ks, half).transpose(0, 2, 1)
     vmem = pl.BlockSpec(memory_space=pltpu.VMEM)
     return pl.pallas_call(
         kernel,
@@ -497,9 +506,12 @@
             jax.ShapeDtypeStruct((tokens, ks), BF16),
             jax.ShapeDtypeStruct((half, ks), F32),
         ),
-        in_specs=[vmem] * 6,
+        in_specs=[vmem] * 4 + [pl.BlockSpec(memory_space=pl.ANY)],
         out_specs=(vmem, vmem),
         scratch_shapes=[
+            pltpu.VMEM((4 * ks, 256), BF16),
+            pltpu.VMEM((4, half, ks), BF16),
+            pltpu.VMEM((ks, tokens), BF16),
             pltpu.VMEM((32, width, depth), BF16),
             pltpu.VMEM((tokens, depth), BF16),
             pltpu.VMEM((tokens, kt), BF16),
@@ -520,17 +532,17 @@
             pltpu.VMEM((2, 2, half, cols), BF16),
             pltpu.SemaphoreType.DMA((SLOTS,)),
             pltpu.SemaphoreType.DMA((SLOTS,)),
+            pltpu.SemaphoreType.DMA,
         ],
         compiler_params=pltpu.CompilerParams(
             collective_id=0, has_side_effects=True, vmem_limit_bytes=60 * 2**20
         ),
     )(
         teacher_rows,
-        teacher_gain.reshape(1, kt),
+        teacher_gain,
         projector.T,
-        weight_t,
         student_rows,
-        student_rows.T,
+        student_weight,
     )
 
 

time: 179 us -> 170 us (0.950); the launches traced: 175 us -> 169 us
  local copies, waits for them, and re-layouts: 9.6 us -> 3.5 us
    reshape x2 -> x0, local copies, waits for them, and re-layouts: 2.27 us -> none  [the longest x1 1.28 us: shards(): teacher_gain.reshape(1, kt)]
    unnamed x3 -> x2, local copies, waits for them, and re-layouts: 5.61 us -> 3.5 us
where the time goes in v3:
time: 170 us; the launch traced here: 169 us
  Pallas kernels  165 us (97%)
  local copies, waits for them, and re-layouts  3.5 us (2%)
    pallas_call x1, Pallas kernels, shards(): pl.pallas_call(kernel, out_shape=(jax.ShapeDtypeStruct((tokens, ks), BF16...  165 us
    unnamed x2, local copies, waits for them, and re-layouts  3.5 us

profile of v3, /device:TPU:1, one launch (start us, length us, event | category | flops | bytes accessed | tf_op | source)
XLA Modules:
  0.0 169.4 jit_solution(6258524085265210759)
XLA Ops:
  0.6 165.3 %shard_map.68 = (bf16[384,768]{1,0:T(8,128)(2,1)}, f32[48,768]{1,0:T(8,128)}) custom-call(bf16[384,1664]{1,0:T(8,128)(2,1)} %t_ref.1, bf16[1664]{0:T(1024)(128)(2,1)} %g_ref.1, bf16[96,1664]{1,0:T(8,128)(2,1)} %bitcast.1, bf16[384,768]{1,0:T(8,128)(2,1)} %x_ref.1, bf16[3072,768]{1,0:T(8,128)(2,1)} %weight_ref.1), custom_call_target="tpu_custom_call" | custom-call | tf_op jit(solution)/shard_map/pallas_call | solution.py:503
  165.9 1.9 %copy.9 = bf16[384,768]{1,0:T(8,128)(2,1)} copy(bf16[384,768]{1,0:T(8,128)(2,1)} %get-tuple-element.4) | data formatting | bytes 1179648
  167.8 1.6 copy.10

commit v4 on v3

--- a/solution.py
+++ b/solution.py
@@ -14,13 +14,13 @@
 GATHER = 0
 ZSWAP = 40
 WEIGHT = 41
-SQUARES = 49
-PAIRED = 52
-SIBLING = 53
-NARROW_RS = 55
-NARROW_AG = 61
-CORE_SUM = 67
-WIDE_RS = 71
+SQUARES = 45
+PAIRED = 48
+SIBLING = 49
+NARROW_RS = 51
+NARROW_AG = 57
+CORE_SUM = 65
+WIDE_RS = 70
 FINAL = 75
 SLOTS = 79
 
@@ -62,18 +62,18 @@
         for cc in range(2)
     ]
 
-    owner = w // 8
+    holder = n % 2 == y // 2
+    w_slab = at(n // 2, y, x)
     column = 2 * half * (w % 8) + half * c
     low = jnp.minimum(column // 128 * 128, ks - 256)
     fetch = pltpu.make_async_copy(weight_ref.at[:, pl.ds(pl.multiple_of(low, 128), 256)], window, local_sem)
 
-    @pl.when(n == owner)
+    @pl.when(holder)
     def _():
         fetch.start()
 
     barrier = pltpu.get_barrier_semaphore()
-    z_dev = [{"wide": at(1 - zl, y, x), "narrow": (n + d) % 4} for d in range(4)]
-    greeted = [sibling, n_dev[1], n_dev[2], n_dev[3]] + z_dev
+    greeted = [sibling, z_other, n_dev[1], n_dev[2], n_dev[3]]
     for device in greeted:
         pl.semaphore_signal(barrier, inc=1, device_id=device, device_id_type=MESH)
 
@@ -99,19 +99,17 @@
 
     w_cols, p_cols = pl.ds(kt, ks), pl.ds(0, kt)
 
-    def weight_copy(k):
+    def weight_copy(k, plane):
         return pltpu.make_async_remote_copy(
-            src_ref=wt_ref.at[(n + k) % 4], dst_ref=ct.at[w, rows, w_cols], send_sem=send_sem.at[WEIGHT + k],
-            recv_sem=recv_sem.at[WEIGHT + k // 4], device_id=(n_dev[k] if k < 4 else z_dev[k - 4]),
-            device_id_type=MESH,
+            src_ref=wt_ref.at[(n + k) % 4], dst_ref=ct.at[w_slab, rows, w_cols], send_sem=send_sem.at[WEIGHT + k],
+            recv_sem=recv_sem.at[WEIGHT + plane], device_id=n_dev[k], device_id_type=MESH,
         )
 
-    w_other = at(1 - zl, y, x)
     ct[w, rows, p_cols] = pt_ref[rows, :]
     z_copy = copy(ct.at[w, rows, p_cols], ct.at[w, rows, p_cols], ZSWAP, z_other)
     z_copy.start()
 
-    @pl.when(n == owner)
+    @pl.when(holder)
     def _():
         fetch.wait()
         row = lax.broadcasted_iota(jnp.int32, (half, 256), 0)
@@ -121,9 +119,98 @@
             wt_ref[q] = lax.dot_general(
                 pick, window[ks * q : ks * q + ks, :], (((1,), (1,)), ((), ())), preferred_element_type=F32
             ).astype(BF16)
-        for k in (1, 5, 2, 6, 3, 7, 4):
-            weight_copy(k).start()
-        ct[w, rows, w_cols] = wt_ref[n]
+        for k in (2, 1, 3):
+            weight_copy(k, n // 2).start()
+        ct[w_slab, rows, w_cols] = wt_ref[n]
+
+    def weight_arrives(plane):
+        @pl.when(n != 2 * plane + y // 2)
+        def _():
+            weight_copy(1, plane).wait_recv()
+
+        @pl.when(zl != plane)
+        def _():
+            z_copy.wait_recv()
+
+    def slab(index, part=None):
+        if part is None:
+            return ct.at[index, rows]
+        return ct.at[index, rows, pl.ds(0, cut) if part == 0 else pl.ds(cut, depth - cut)]
+
+    def spread(index, slot, device, part=None):
+        return copy(slab(index, part), slab(index, part), slot, device)
+
+    sent = []
+
+    def go(item):
+        item.start()
+        sent.append(item)
+
+    along_a, along_b = jnp.where(c == 0, x, y), jnp.where(c == 0, y, x)
+
+    def cell(plane, da, db):
+        a, b = (along_a + da) % 4, (along_b + db) % 4
+        return plane * 16 + jnp.where(c == 0, 4 * b + a, 4 * a + b)
+
+    first = [{"wide": cell(zl, 1, 0)}, {"wide": cell(zl, 3, 0)}, {"wide": cell(zl, 2, 0)}]
+    second = [{"wide": cell(zl, 0, 1)}, {"wide": cell(zl, 0, 3)}]
+    ALONG = (0, 3, 1, 2)
+
+    class Plane:
+        def __init__(self, p, plane):
+            self.base, self.p, self.plane = GATHER + 20 * p, p, plane
+
+        def to_sibling(self, index):
+            copy(slab(index), slab(index), SIBLING + self.p, sibling).start()
+
+        def whole(self):
+            planes = ct.at[pl.ds(16 * self.plane, 16), rows]
+            return copy(planes, planes, SIBLING + self.p, sibling)
+
+        def begin(self):
+            weight_arrives(self.plane)
+            own = cell(self.plane, 0, 0)
+            for side in range(3):
+                go(spread(own, self.base + side, first[side]))
+            self.second_send(0)
+            self.to_sibling(own)
+
+        def second_send(self, j):
+            index = cell(self.plane, ALONG[j], 0)
+            for side in range(2):
+                go(spread(index, self.base + 4 + 4 * j + side, second[side]))
+
+        def first_near(self):
+            for side in range(2):
+                index = cell(self.plane, ALONG[1 + side], 0)
+                spread(index, self.base + side, first[side]).wait_recv()
+                self.second_send(1 + side)
+                self.to_sibling(index)
+
+        def first_far(self):
+            index = cell(self.plane, 2, 0)
+            spread(index, self.base + 2, first[2]).wait_recv()
+            self.second_send(3)
+            self.to_sibling(index)
+
+        def second_near(self, j):
+            slot = self.base + 4 + 4 * j
+            for side in range(2):
+                index = cell(self.plane, ALONG[j], 3 if side == 0 else 1)
+                spread(index, slot + side, second[side]).wait_recv()
+                go(spread(index, slot + 2 + side, second[side], side))
+                self.to_sibling(index)
+
+        def second_far(self, j):
+            slot = self.base + 4 + 4 * j
+            index = cell(self.plane, ALONG[j], 2)
+            for side in range(2):
+                spread(index, slot + 2 + side, second[side], side).wait_recv()
+            self.to_sibling(index)
+
+    p_first = 1 - n // 2
+    near_plane, far_plane = Plane(0, p_first), Plane(1, 1 - p_first)
+    near_plane.begin()
 
     eye = lax.broadcasted_iota(jnp.int32, (128, 128), 0) == lax.broadcasted_iota(jnp.int32, (128, 128), 1)
     groups = tokens // 128
@@ -135,96 +222,6 @@
     sq_copies = [copy(sq.at[0], sq.at[d], SQUARES + d - 1, n_dev[d]) for d in (1, 2, 3)]
     for item in sq_copies:
         item.start()
-
-    def weight_arrives(plane):
-        @pl.when(jnp.logical_and(zl == plane, n != owner))
-        def _():
-            weight_copy(1).wait_recv()
-
-        @pl.when(zl != plane)
-        def _():
-            weight_copy(5).wait_recv()
-            z_copy.wait_recv()
-
-    def slab(index, part=None):
-        if part is None:
-            return ct.at[index, rows]
-        return ct.at[index, rows, pl.ds(0, cut) if part == 0 else pl.ds(cut, depth - cut)]
-
-    def spread(index, slot, device, part=None):
-        return copy(slab(index, part), slab(index, part), slot, device)
-
-    sent = []
-
-    def go(item):
-        item.start()
-        sent.append(item)
-
-    along_a, along_b = jnp.where(c == 0, x, y), jnp.where(c == 0, y, x)
-
-    def cell(plane, da, db):
-        a, b = (along_a + da) % 4, (along_b + db) % 4
-        return plane * 16 + jnp.where(c == 0, 4 * b + a, 4 * a + b)
-
-    first = [{"wide": cell(zl, 1, 0)}, {"wide": cell(zl, 3, 0)}, {"wide": cell(zl, 2, 0)}]
-    second = [{"wide": cell(zl, 0, 1)}, {"wide": cell(zl, 0, 3)}]
-    ALONG = (0, 3, 1, 2)
-
-    class Plane:
-        def __init__(self, p, plane):
-            self.base, self.p, self.plane = GATHER + 20 * p, p, plane
-
-        def to_sibling(self, index):
-            copy(slab(index), slab(index), SIBLING + self.p, sibling).start()
-
-        def whole(self):
-            planes = ct.at[pl.ds(16 * self.plane, 16), rows]
-            return copy(planes, planes, SIBLING + self.p, sibling)
-
-        def begin(self):
-            weight_arrives(self.plane)
-            own = cell(self.plane, 0, 0)
-            for side in range(3):
-                go(spread(own, self.base + side, first[side]))
-            self.second_send(0)
-            self.to_sibling(own)
-
-        def second_send(self, j):
-            index = cell(self.plane, ALONG[j], 0)
-            for side in range(2):
-                go(spread(index, self.base + 4 + 4 * j + side, second[side]))
-
-        def first_near(self):
-            for side in range(2):
-                index = cell(self.plane, ALONG[1 + side], 0)
-                spread(index, self.base + side, first[side]).wait_recv()
-                self.second_send(1 + side)
-                self.to_sibling(index)
-
-        def first_far(self):
-            index = cell(self.plane, 2, 0)
-            spread(index, self.base + 2, first[2]).wait_recv()
-            self.second_send(3)
-            self.to_sibling(index)
-
-        def second_near(self, j):
-            slot = self.base + 4 + 4 * j
-            for side in range(2):
-                index = cell(self.plane, ALONG[j], 3 if side == 0 else 1)
-                spread(index, slot + side, second[side]).wait_recv()
-                go(spread(index, slot + 2 + side, second[side], side))
-                self.to_sibling(index)
-
-        def second_far(self, j):
-            slot = self.base + 4 + 4 * j
-            index = cell(self.plane, ALONG[j], 2)
-            for side in range(2):
-                spread(index, slot + 2 + side, second[side], side).wait_recv()
-            self.to_sibling(index)
-
-    p_first = 1 - n // 2
-    near_plane, far_plane = Plane(0, p_first), Plane(1, 1 - p_first)
-    near_plane.begin()
 
     lhs[:, kt:] = x_ref[...]
     xt_ref[...] = x_ref[...].T
@@ -320,14 +317,15 @@
 
     lax.fori_loop(0, 2, own_block, 0)
 
-    def ag(block, h, e, slot):
-        return copy(m.at[block, h], m.at[block, h], NARROW_AG + slot, by(e))
+    wide_part = 2 * cols // 3
+    PARTS = (pl.ds(0, wide_part), pl.ds(wide_part, cols - wide_part))
 
     def own_copy(h, e):
-        return ag(n, h, e, 2 * e + h)
-
-    def pass_on(e):
-        return ag((n + 3 + 2 * e) % 4, e, e, 4 + e)
+        return copy(m.at[n, h], m.at[n, h], NARROW_AG + 2 * e + h, by(e))
+
+    def pass_on(e, s):
+        piece = m.at[(n + 3 + 2 * e) % 4, e, :, PARTS[s]]
+        return copy(piece, piece, NARROW_AG + 4 + 2 * e + s, by(e))
 
     early_copy(e2).wait_recv()
     late_copy(e2).wait_recv()
@@ -350,26 +348,48 @@
 
     lax.fori_loop(0, 2, finish, 0)
     igacc[...] = jnp.zeros((tokens, ks), F32)
-
-    def core_copy(d):
-        return copy(core_out.at[d], core_in.at[d], CORE_SUM + d, sibling)
-
     me = 4 * y + x
 
-    def wide_send(d):
+    def core_copy(d, columns, slot):
+        return copy(core_out.at[d, :, columns], core_in.at[d, :, columns], CORE_SUM + slot, sibling)
+
+    def wide_send(d, columns, slot):
         def one(k, carry):
             yy, xx = peer(k)
             copy(
-                wide_out.at[d, 4 * yy + xx], wide_in.at[d, me], WIDE_RS + d, {"wide": at(zl, yy, xx)}
+                wide_out.at[d, 4 * yy + xx, :, columns], wide_in.at[d, me, :, columns], WIDE_RS + slot,
+                {"wide": at(zl, yy, xx)},
             ).start()
             return carry
 
         lax.fori_loop(1, 16, one, 0)
 
-    def wide_all(d):
+    def wide_all(d, columns, slot):
         return copy(
-            wide_out.at[d, pl.ds(0, 15)], wide_in.at[d, pl.ds(0, 15)], WIDE_RS + d, {"wide": at(zl, y, (x + 1) % 4)}
+            wide_out.at[d, pl.ds(0, 15), :, columns], wide_in.at[d, pl.ds(0, 15), :, columns], WIDE_RS + slot,
+            {"wide": at(zl, y, (x + 1) % 4)},
         )
+
+    def gradient(d, columns, slot):
+        b = (n + d) % 4
+        core_out[d, :, columns] = jnp.dot(
+            xt_ref[...], m[b, 1 - c, :, columns], preferred_element_type=F32
+        ).astype(BF16)
+        core_copy(d, columns, slot).start()
+        kept[:, columns] = jnp.dot(xt_ref[...], m[b, c, :, columns], preferred_element_type=F32)
+
+    def chip_sum(d, columns, slot):
+        core_copy(d, columns, slot).wait_recv()
+        both = (kept[:, columns] + core_in[d, :, columns].astype(F32)).astype(BF16)
+        wide_out[d, :, :, columns] = both.reshape(16, half, columns.size)
+        wide_in[d, me, :, columns] = wide_out[d, me, :, columns]
+        wide_send(d, columns, slot)
+
+    def backward(d):
+        b = (n + d) % 4
+        for h in range(2):
+            block = ct[pl.ds(8 * b + 4 * h, 4), :, pl.ds(kt, ks)].reshape(cols, ks)
+            igacc[...] += jnp.dot(m[b, h], block, preferred_element_type=F32)
 
     def final_copy(d):
         return pltpu.make_async_remote_copy(
@@ -378,7 +398,6 @@
         )
 
     def reduce(d):
-        wide_all(d).wait_recv()
         total = wide_in[d, 0].astype(F32)
         for k in range(1, 16):
             total = total + wide_in[d, k].astype(F32)
@@ -393,82 +412,33 @@
             fin_out[d] = total.astype(BF16)
             final_copy(d).start()
 
-    def order(r):
-        return jnp.where(r == 0, 0, jnp.where(r == 1, 3, jnp.where(r == 2, 1, 2)))
-
-    def backward(i, carry):
-        r = i // 2
-
-        @pl.when(i == 2)
+    ALL = pl.ds(0, cols)
+
+    def near_gradient(r, carry):
+        @pl.when(r == 1)
         def _():
             own_copy(0, 0).wait_recv()
-            pass_on(0).start()
+            pass_on(0, 0).start()
+            pass_on(0, 1).start()
             own_copy(1, 1).wait_recv()
-            pass_on(1).start()
+            pass_on(1, 0).start()
+            pass_on(1, 1).start()
             own_copy(1, 0).wait_recv()
 
-        @pl.when(i == 4)
+        @pl.when(r == 2)
         def _():
             own_copy(0, 1).wait_recv()
 
-        @pl.when(i == 6)
-        def _():
-            reduce(0)
-            pass_on(0).wait_recv()
-            pass_on(1).wait_recv()
-
-        d = order(r)
-        h = jnp.where(i % 2 == 0, 1 - c, c)
-        b = (n + d) % 4
-        piece = m[b, h]
-        block = ct[pl.ds(8 * b + 4 * h, 4), :, pl.ds(kt, ks)].reshape(cols, ks)
-        grad = jnp.dot(xt_ref[...], piece, preferred_element_type=F32)
-
-        @pl.when(i % 2 == 0)
-        def _():
-            core_out[d] = grad.astype(BF16)
-            core_copy(d).start()
-
-        @pl.when(i % 2 == 1)
-        def _():
-            kept[...] = grad
-
-        igacc[...] += jnp.dot(piece, block, preferred_element_type=F32)
-
-        @pl.when(i % 2 == 1)
-        def _():
-            core_copy(d).wait_recv()
-            both = (kept[...] + core_in[d].astype(F32)).astype(BF16).reshape(16, half, cols)
-            wide_out[d] = both
-            wide_in[d, me] = wide_out[d, me]
-            wide_send(d)
-
+        d = jnp.where(r == 0, 0, jnp.where(r == 1, 3, 1))
+        slot = jnp.where(d == 3, 2, d)
+        gradient(d, ALL, slot)
+        backward(d)
+        chip_sum(d, ALL, slot)
         return carry
 
-    lax.fori_loop(0, 8, backward, 0)
-    for h in range(2):
-        span = slice(cols * h, cols * h + cols)
-        ig_ref[:, span] = (m[n, h].astype(F32) + igacc[:, span]).astype(BF16)
-
-    def reduce_rest(r, carry):
-        reduce(order(r))
-        return carry
-
-    lax.fori_loop(1, 4, reduce_rest, 0)
-    scale = 1.0 / (tokens * 64.0) ** 0.5
-    for zz in range(2):
-        for cc in range(2):
-
-            @pl.when(jnp.logical_not(sources[2 * zz + cc][1]))
-            def _():
-                pltpu.make_async_remote_copy(
-                    src_ref=fin_out.at[0], dst_ref=fin_in.at[zz, cc], send_sem=send_sem.at[FINAL],
-                    recv_sem=recv_sem.at[FINAL + 2 * zz + cc], device_id=sibling, device_id_type=MESH,
-                ).wait_recv()
-
-    for h in range(2):
-        wg_ref[:, cols * h : cols * h + cols] = (fin_in[0, h].astype(F32) + fin_in[1, h].astype(F32)) * scale
-
+    lax.fori_loop(0, 3, near_gradient, 0)
+    wide_all(0, ALL, 0).wait_recv()
+    reduce(0)
     for item in sent + sq_copies + [z_copy]:
         item.wait_send()
     near_plane.whole().wait_send()
@@ -477,21 +447,58 @@
         far_copy(e).wait_send()
         early_copy(e).wait_send()
         late_copy(e).wait_send()
-        pass_on(e).wait_send()
-        for h in range(2):
-            own_copy(h, e).wait_send()
-    for d in range(4):
-        core_copy(d).wait_send()
-        wide_all(d).wait_send()
-
-        @pl.when(jnp.logical_not(jnp.logical_and(at_home, d == 0)))
-        def _():
-            final_copy(d).wait_send()
-
-    @pl.when(n == owner)
+
+    @pl.when(holder)
     def _():
-        for k in range(1, 8):
-            weight_copy(k).wait_send()
+        for k in range(1, 4):
+            weight_copy(k, n // 2).wait_send()
+
+    for s in range(2):
+        for e in range(2):
+            pass_on(e, s).wait_recv()
+        gradient(2, PARTS[s], 3 + s)
+        chip_sum(2, PARTS[s], 3 + s)
+    backward(2)
+    for h in range(2):
+        span = slice(cols * h, cols * h + cols)
+        ig_ref[:, span] = (m[n, h].astype(F32) + igacc[:, span]).astype(BF16)
+    wide_all(3, ALL, 2).wait_recv()
+    reduce(3)
+    wide_all(1, ALL, 1).wait_recv()
+    reduce(1)
+    for s in range(2):
+        wide_all(2, PARTS[s], 3 + s).wait_recv()
+    reduce(2)
+
+    def late_waits():
+        for e in range(2):
+            for k in range(2):
+                pass_on(e, k).wait_send()
+                own_copy(k, e).wait_send()
+        for d, columns, slot in ((0, ALL, 0), (1, ALL, 1), (3, ALL, 2), (2, PARTS[0], 3), (2, PARTS[1], 4)):
+            core_copy(d, columns, slot).wait_send()
+            wide_all(d, columns, slot).wait_send()
+        for d in range(4):
+
+            @pl.when(jnp.logical_not(jnp.logical_and(at_home, d == 0)))
+            def _():
+                final_copy(d).wait_send()
+
+    scale = 1.0 / (tokens * 64.0) ** 0.5
+    for zz in range(2):
+        for cc in range(2):
+
+            @pl.when(jnp.logical_not(sources[2 * zz + cc][1]))
+            def _():
+                pltpu.make_async_remote_copy(
+                    src_ref=fin_out.at[0], dst_ref=fin_in.at[zz, cc], send_sem=send_sem.at[FINAL],
+                    recv_sem=recv_sem.at[FINAL + 2 * zz + cc], device_id=sibling, device_id_type=MESH,
+                ).wait_recv()
+
+    for h in range(2):
+        wg_ref[:, cols * h : cols * h + cols] = (fin_in[0, h].astype(F32) + fin_in[1, h].astype(F32)) * scale
+
+    late_waits()
 
 
 def shards(teacher_rows, teacher_gain, projector, student_rows, student_weight):

time: 170 us -> 178 us (1.047)
  the two profiles are of different devices: /device:TPU:1 before, /device:TPU:97 now
where the time goes in v4:
time: 178 us; the launch traced here: 177 us
  Pallas kernels  173 us (97%)
  local copies, waits for them, and re-layouts  3.5 us (2%)
    pallas_call x1, Pallas kernels, shards(): pl.pallas_call(kernel, out_shape=(jax.ShapeDtypeStruct((tokens, ks), BF16...  173 us

profile of v4, /device:TPU:97, one launch (start us, length us, event | category | flops | bytes accessed | tf_op | source)
XLA Modules:
  0.0 177.4 jit_solution(1634403994591594863)
XLA Ops:
  0.6 173.2 %shard_map.68 = (bf16[384,768]{1,0:T(8,128)(2,1)}, f32[48,768]{1,0:T(8,128)}) custom-call(bf16[384,1664]{1,0:T(8,128)(2,1)} %t_ref.1, bf16[1664]{0:T(1024)(128)(2,1)} %g_ref.1, bf16[96,1664]{1,0:T(8,128)(2,1)} %bitcast.1, bf16[384,768]{1,0:T(8,128)(2,1)} %x_ref.1, bf16[3072,768]{1,0:T(8,128)(2,1)} %weight_ref.1), custom_call_target="tpu_custom_call" | custom-call | tf_op jit(solution)/shard_map/pallas_call | solution.py:510
  173.9 1.9 %copy.9 = bf16[384,768]{1,0:T(8,128)(2,1)} copy(bf16[384,768]{1,0:T(8,128)(2,1)} %get-tuple-element.4) | data formatting | bytes 1179648
  175.8 1.6 copy.10

commit v5 on v4

--- a/solution.py
+++ b/solution.py
@@ -27,7 +27,7 @@
 
 def kernel(
     t_ref, g_ref, pt_ref, x_ref, weight_ref, ig_ref, wg_ref, window, wt_ref, xt_ref,
-    ct, lhs, hid, sq, part, far_out, near_out, far_in, near_in, m, igacc,
+    ct, lhs, hid, sq, inverse, part, far_out, near_out, far_in, near_in, m, igacc,
     kept, core_out, core_in, wide_out, wide_in, fin_out, fin_in, send_sem, recv_sem, local_sem,
 ):
     c = lax.axis_index("section")
@@ -115,10 +115,15 @@
         row = lax.broadcasted_iota(jnp.int32, (half, 256), 0)
         lane = lax.broadcasted_iota(jnp.int32, (half, 256), 1)
         pick = jnp.where(lane == row + (column - low), 1.0, 0.0).astype(BF16)
-        for q in range(4):
+
+        def transpose(q, carry):
+            span = pl.ds(pl.multiple_of(ks * q, ks), ks)
             wt_ref[q] = lax.dot_general(
-                pick, window[ks * q : ks * q + ks, :], (((1,), (1,)), ((), ())), preferred_element_type=F32
+                pick, window[span, :], (((1,), (1,)), ((), ())), preferred_element_type=F32
             ).astype(BF16)
+            return carry
+
+        lax.fori_loop(0, 4, transpose, 0)
         for k in (2, 1, 3):
             weight_copy(k, n // 2).start()
         ct[w_slab, rows, w_cols] = wt_ref[n]
@@ -140,11 +145,8 @@
     def spread(index, slot, device, part=None):
         return copy(slab(index, part), slab(index, part), slot, device)
 
-    sent = []
-
-    def go(item):
+    def start(item):
         item.start()
-        sent.append(item)
 
     along_a, along_b = jnp.where(c == 0, x, y), jnp.where(c == 0, y, x)
 
@@ -171,14 +173,14 @@
             weight_arrives(self.plane)
             own = cell(self.plane, 0, 0)
             for side in range(3):
-                go(spread(own, self.base + side, first[side]))
+                start(spread(own, self.base + side, first[side]))
             self.second_send(0)
             self.to_sibling(own)
 
         def second_send(self, j):
             index = cell(self.plane, ALONG[j], 0)
             for side in range(2):
-                go(spread(index, self.base + 4 + 4 * j + side, second[side]))
+                start(spread(index, self.base + 4 + 4 * j + side, second[side]))
 
         def first_near(self):
             for side in range(2):
@@ -198,7 +200,7 @@
             for side in range(2):
                 index = cell(self.plane, ALONG[j], 3 if side == 0 else 1)
                 spread(index, slot + side, second[side]).wait_recv()
-                go(spread(index, slot + 2 + side, second[side], side))
+                start(spread(index, slot + 2 + side, second[side], side))
                 self.to_sibling(index)
 
         def second_far(self, j):
@@ -208,6 +210,14 @@
                 spread(index, slot + 2 + side, second[side], side).wait_recv()
             self.to_sibling(index)
 
+        def wait_sends(self):
+            for side in range(3):
+                spread(0, self.base + side, first[0]).wait_send()
+            for j in range(4):
+                for side in range(2):
+                    spread(0, self.base + 4 + 4 * j + side, first[0]).wait_send()
+                    spread(0, self.base + 6 + 4 * j + side, first[0], side).wait_send()
+
     p_first = 1 - n // 2
     near_plane, far_plane = Plane(0, p_first), Plane(1, 1 - p_first)
     near_plane.begin()
@@ -215,36 +225,45 @@
     eye = lax.broadcasted_iota(jnp.int32, (128, 128), 0) == lax.broadcasted_iota(jnp.int32, (128, 128), 1)
     groups = tokens // 128
     sq[0] = jnp.zeros((8, 128), F32)
-    for i in range(groups):
-        part_t = t_ref[128 * i : 128 * i + 128, :].astype(F32)
+
+    def squares(i, carry):
+        part_t = t_ref[pl.ds(pl.multiple_of(128 * i, 128), 128), :].astype(F32)
         col = jnp.sum(part_t * part_t, axis=1, keepdims=True)
-        sq[0, i : i + 1, :] = jnp.sum(jnp.where(eye, col, 0.0), axis=0, keepdims=True)
+        sq[0, pl.ds(i, 1), :] = jnp.sum(jnp.where(eye, col, 0.0), axis=0, keepdims=True)
+        return carry
+
+    lax.fori_loop(0, groups, squares, 0)
     sq_copies = [copy(sq.at[0], sq.at[d], SQUARES + d - 1, n_dev[d]) for d in (1, 2, 3)]
     for item in sq_copies:
         item.start()
 
-    lhs[:, kt:] = x_ref[...]
-    xt_ref[...] = x_ref[...].T
     for item in sq_copies:
         item.wait_recv()
-    inverse = lax.rsqrt((sq[0] + sq[1] + sq[2] + sq[3]) / (4 * kt) + 1e-05)
-    gain = g_ref[...].astype(F32).reshape(1, kt)
-    for i in range(groups):
-        col = jnp.sum(jnp.where(eye, inverse[i : i + 1, :], 0.0), axis=1, keepdims=True)
-        span = slice(128 * i, 128 * i + 128)
+    inverse[...] = lax.rsqrt((sq[0] + sq[1] + sq[2] + sq[3]) / (4 * kt) + 1e-05)
+
+    def normalize(i, carry):
+        span = pl.ds(pl.multiple_of(128 * i, 128), 128)
+        col = jnp.sum(jnp.where(eye, inverse[pl.ds(i, 1), :], 0.0), axis=1, keepdims=True)
+        gain = g_ref[...].astype(F32).reshape(1, kt)
         hid[span, :] = -(t_ref[span, :].astype(F32) * col * gain).astype(BF16)
+        lhs[span, pl.ds(kt, ks)] = x_ref[span, :]
+        xt_ref[:, span] = x_ref[span, :].T
+        return carry
+
+    lax.fori_loop(0, groups, normalize, 0)
     paired_copy = copy(hid, lhs.at[:, pl.ds(0, kt)], PAIRED, sibling)
-    go(paired_copy)
+    paired_copy.start()
 
     near_plane.first_near()
     near_plane.second_near(0)
     near_plane.first_far()
     near_plane.second_near(1)
     near_plane.second_far(0)
+    far_plane.begin()
     near_plane.second_near(2)
     near_plane.second_far(1)
-    far_plane.begin()
     near_plane.second_near(3)
+    far_plane.first_near()
     near_plane.second_far(2)
     near_plane.second_far(3)
     paired_copy.wait_recv()
@@ -269,63 +288,65 @@
         block = ct[pl.ds(8 * b + 4 * h, 4)].reshape(cols, depth)
         return lax.dot_general(lhs[...], block, (((1,), (1,)), ((), ())), preferred_element_type=F32)
 
-    def far_block(e, carry):
-        far_out[e] = product((n + 2) % 4, e).astype(BF16)
-        far_copy(e).start()
-        return carry
-
-    def near_block(e):
-        def step(k, carry):
-            h = jnp.where(k == 0, 1 - e, e)
-            part[h] = product((n + 1 + 2 * e) % 4, h)
-
-            @pl.when(k == 0)
-            def _():
-                near_out[e, h] = part[h].astype(BF16)
-                early_copy(e).start()
-
-            return carry
-
-        lax.fori_loop(0, 2, step, 0)
-
     def send_late(e):
         far_copy(e).wait_recv()
         near_out[e, e] = (part[e] + far_in[e].astype(F32)).astype(BF16)
         late_copy(e).start()
 
-    lax.fori_loop(0, 2, far_block, 0)
-    far_plane.first_near()
-    near_block(e1)
-    far_plane.second_near(0)
-    far_plane.first_far()
-    far_plane.second_near(1)
-    far_plane.second_far(0)
-    far_plane.second_near(2)
-    far_plane.second_far(1)
-    far_plane.second_near(3)
-    send_late(e1)
-    far_plane.second_far(2)
-    far_plane.second_far(3)
-    far_plane.whole().wait_recv()
-    near_block(e2)
-    send_late(e2)
-
-    def own_block(h, carry):
-        span = pl.ds(pl.multiple_of(cols * h, cols), cols)
-        part[h] = product(n, h) + x_ref[:, span].astype(F32)
-        return carry
-
-    lax.fori_loop(0, 2, own_block, 0)
-
-    wide_part = 2 * cols // 3
-    PARTS = (pl.ds(0, wide_part), pl.ds(wide_part, cols - wide_part))
+    def products(i, carry):
+        r, k = i // 2, i % 2
+
+        @pl.when(i == 2)
+        def _():
+            far_plane.second_near(0)
+            far_plane.first_far()
+
+        @pl.when(i == 4)
+        def _():
+            far_plane.second_near(1)
+            far_plane.second_far(0)
+            far_plane.second_near(2)
+            far_plane.second_far(1)
+            far_plane.second_near(3)
+
+        @pl.when(jnp.logical_or(i == 4, i == 6))
+        def _():
+            send_late(jnp.where(i == 4, e1, e2))
+
+        @pl.when(i == 4)
+        def _():
+            far_plane.second_far(2)
+            far_plane.second_far(3)
+            far_plane.whole().wait_recv()
+
+        e = jnp.where(r == 1, e1, e2)
+        beside = jnp.logical_or(r == 1, r == 2)
+        b = (n + jnp.where(r == 0, 2, jnp.where(r == 3, 0, 1 + 2 * e))) % 4
+        h = jnp.where(beside, jnp.where(k == 0, 1 - e, e), k)
+        early = jnp.logical_and(beside, k == 0)
+        part[h] = product(b, h)
+
+        @pl.when(r == 0)
+        def _():
+            far_out[k] = part[h].astype(BF16)
+            far_copy(k).start()
+
+        @pl.when(early)
+        def _():
+            near_out[e, h] = part[h].astype(BF16)
+            early_copy(e).start()
+
+        return carry
+
+    lax.fori_loop(0, 8, products, 0)
+
 
     def own_copy(h, e):
         return copy(m.at[n, h], m.at[n, h], NARROW_AG + 2 * e + h, by(e))
 
-    def pass_on(e, s):
-        piece = m.at[(n + 3 + 2 * e) % 4, e, :, PARTS[s]]
-        return copy(piece, piece, NARROW_AG + 4 + 2 * e + s, by(e))
+    def pass_on(e):
+        piece = m.at[(n + 3 + 2 * e) % 4, e]
+        return copy(piece, piece, NARROW_AG + 4 + e, by(e))
 
     early_copy(e2).wait_recv()
     late_copy(e2).wait_recv()
@@ -341,7 +362,9 @@
         def _():
             late_copy(e1).wait_recv()
 
-        m[n, h] = (part[h] + near_in[0, h].astype(F32) + near_in[1, h].astype(F32)).astype(BF16)
+        span = pl.ds(pl.multiple_of(cols * h, cols), cols)
+        own = part[h] + x_ref[:, span].astype(F32)
+        m[n, h] = (own + near_in[0, h].astype(F32) + near_in[1, h].astype(F32)).astype(BF16)
         own_copy(h, 0).start()
         own_copy(h, 1).start()
         return carry
@@ -350,46 +373,30 @@
     igacc[...] = jnp.zeros((tokens, ks), F32)
     me = 4 * y + x
 
-    def core_copy(d, columns, slot):
-        return copy(core_out.at[d, :, columns], core_in.at[d, :, columns], CORE_SUM + slot, sibling)
-
-    def wide_send(d, columns, slot):
+    def core_copy(d):
+        return copy(core_out.at[d], core_in.at[d], CORE_SUM + d, sibling)
+
+    def wide_send(d):
         def one(k, carry):
             yy, xx = peer(k)
             copy(
-                wide_out.at[d, 4 * yy + xx, :, columns], wide_in.at[d, me, :, columns], WIDE_RS + slot,
-                {"wide": at(zl, yy, xx)},
+                wide_out.at[d, 4 * yy + xx], wide_in.at[d, me], WIDE_RS + d, {"wide": at(zl, yy, xx)}
             ).start()
             return carry
 
         lax.fori_loop(1, 16, one, 0)
 
-    def wide_all(d, columns, slot):
+    def wide_all(d):
         return copy(
-            wide_out.at[d, pl.ds(0, 15), :, columns], wide_in.at[d, pl.ds(0, 15), :, columns], WIDE_RS + slot,
-            {"wide": at(zl, y, (x + 1) % 4)},
+            wide_out.at[d, pl.ds(0, 15)], wide_in.at[d, pl.ds(0, 15)], WIDE_RS + d, {"wide": at(zl, y, (x + 1) % 4)}
         )
 
-    def gradient(d, columns, slot):
-        b = (n + d) % 4
-        core_out[d, :, columns] = jnp.dot(
-            xt_ref[...], m[b, 1 - c, :, columns], preferred_element_type=F32
-        ).astype(BF16)
-        core_copy(d, columns, slot).start()
-        kept[:, columns] = jnp.dot(xt_ref[...], m[b, c, :, columns], preferred_element_type=F32)
-
-    def chip_sum(d, columns, slot):
-        core_copy(d, columns, slot).wait_recv()
-        both = (kept[:, columns] + core_in[d, :, columns].astype(F32)).astype(BF16)
-        wide_out[d, :, :, columns] = both.reshape(16, half, columns.size)
-        wide_in[d, me, :, columns] = wide_out[d, me, :, columns]
-        wide_send(d, columns, slot)
-
-    def backward(d):
-        b = (n + d) % 4
-        for h in range(2):
-            block = ct[pl.ds(8 * b + 4 * h, 4), :, pl.ds(kt, ks)].reshape(cols, ks)
-            igacc[...] += jnp.dot(m[b, h], block, preferred_element_type=F32)
+    def chip_sum(d):
+        core_copy(d).wait_recv()
+        both = (kept[...] + core_in[d].astype(F32)).astype(BF16)
+        wide_out[d] = both.reshape(16, half, cols)
+        wide_in[d, me] = wide_out[d, me]
+        wide_send(d)
 
     def final_copy(d):
         return pltpu.make_async_remote_copy(
@@ -398,6 +405,7 @@
         )
 
     def reduce(d):
+        wide_all(d).wait_recv()
         total = wide_in[d, 0].astype(F32)
         for k in range(1, 16):
             total = total + wide_in[d, k].astype(F32)
@@ -412,73 +420,79 @@
             fin_out[d] = total.astype(BF16)
             final_copy(d).start()
 
-    ALL = pl.ds(0, cols)
-
-    def near_gradient(r, carry):
-        @pl.when(r == 1)
+    def backward(i, carry):
+        @pl.when(i == 2)
         def _():
             own_copy(0, 0).wait_recv()
-            pass_on(0, 0).start()
-            pass_on(0, 1).start()
+            pass_on(0).start()
             own_copy(1, 1).wait_recv()
-            pass_on(1, 0).start()
-            pass_on(1, 1).start()
+            pass_on(1).start()
             own_copy(1, 0).wait_recv()
 
-        @pl.when(r == 2)
+        @pl.when(i == 4)
         def _():
             own_copy(0, 1).wait_recv()
 
-        d = jnp.where(r == 0, 0, jnp.where(r == 1, 3, 1))
-        slot = jnp.where(d == 3, 2, d)
-        gradient(d, ALL, slot)
-        backward(d)
-        chip_sum(d, ALL, slot)
-        return carry
-
-    lax.fori_loop(0, 3, near_gradient, 0)
-    wide_all(0, ALL, 0).wait_recv()
-    reduce(0)
-    for item in sent + sq_copies + [z_copy]:
-        item.wait_send()
-    near_plane.whole().wait_send()
-    far_plane.whole().wait_send()
-    for e in range(2):
-        far_copy(e).wait_send()
-        early_copy(e).wait_send()
-        late_copy(e).wait_send()
-
-    @pl.when(holder)
-    def _():
-        for k in range(1, 4):
-            weight_copy(k, n // 2).wait_send()
-
-    for s in range(2):
+        @pl.when(i == 6)
+        def _():
+            early_waits()
+            pass_on(0).wait_recv()
+            pass_on(1).wait_recv()
+
+        r = i // 2
+        d = jnp.where(r == 0, 0, jnp.where(r == 1, 3, jnp.where(r == 2, 1, 2)))
+        h = jnp.where(i % 2 == 0, 1 - c, c)
+        b = (n + d) % 4
+        kept[...] = jnp.dot(xt_ref[...], m[b, h], preferred_element_type=F32)
+
+        @pl.when(i % 2 == 0)
+        def _():
+            core_out[d] = kept[...].astype(BF16)
+            core_copy(d).start()
+
+        block = ct[pl.ds(8 * b + 4 * h, 4), :, pl.ds(kt, ks)].reshape(cols, ks)
+        igacc[...] += jnp.dot(m[b, h], block, preferred_element_type=F32)
+
+        @pl.when(i % 2 == 1)
+        def _():
+            chip_sum(d)
+
+        return carry
+
+    def early_waits():
+        for item in sq_copies + [z_copy, paired_copy, near_plane.whole(), far_plane.whole()]:
+            item.wait_send()
+        near_plane.wait_sends()
+        far_plane.wait_sends()
         for e in range(2):
-            pass_on(e, s).wait_recv()
-        gradient(2, PARTS[s], 3 + s)
-        chip_sum(2, PARTS[s], 3 + s)
-    backward(2)
+            far_copy(e).wait_send()
+            early_copy(e).wait_send()
+            late_copy(e).wait_send()
+
+        @pl.when(holder)
+        def _():
+            for k in range(1, 4):
+                weight_copy(k, n // 2).wait_send()
+
+    lax.fori_loop(0, 8, backward, 0)
     for h in range(2):
         span = slice(cols * h, cols * h + cols)
         ig_ref[:, span] = (m[n, h].astype(F32) + igacc[:, span]).astype(BF16)
-    wide_all(3, ALL, 2).wait_recv()
-    reduce(3)
-    wide_all(1, ALL, 1).wait_recv()
-    reduce(1)
-    for s in range(2):
-        wide_all(2, PARTS[s], 3 + s).wait_recv()
-    reduce(2)
+
+    def reduce_all(r, carry):
+        reduce(jnp.where(r == 1, 3, jnp.where(r == 2, 1, 2 * (r // 3))))
+        return carry
+
+    lax.fori_loop(0, 4, reduce_all, 0)
 
     def late_waits():
         for e in range(2):
-            for k in range(2):
-                pass_on(e, k).wait_send()
-                own_copy(k, e).wait_send()
-        for d, columns, slot in ((0, ALL, 0), (1, ALL, 1), (3, ALL, 2), (2, PARTS[0], 3), (2, PARTS[1], 4)):
-            core_copy(d, columns, slot).wait_send()
-            wide_all(d, columns, slot).wait_send()
+            pass_on(e).wait_send()
+            for h in range(2):
+                own_copy(h, e).wait_send()
         for d in range(4):
+            core_copy(d).wait_send()
+            wide_all(d).wait_send()
 
             @pl.when(jnp.logical_not(jnp.logical_and(at_home, d == 0)))
             def _():
@@ -523,6 +537,7 @@
             pltpu.VMEM((tokens, depth), BF16),
             pltpu.VMEM((tokens, kt), BF16),
             pltpu.VMEM((4, 8, 128), F32),
+            pltpu.VMEM((8, 128), F32),
             pltpu.VMEM((2, tokens, cols), F32),
             pltpu.VMEM((2, tokens, cols), BF16),
             pltpu.VMEM((2, 2, tokens, cols), BF16),

time: 178 us -> 165 us (0.927)
  the two profiles are of different devices: /device:TPU:97 before, /device:TPU:1 now
where the time goes in v5:
time: 165 us
  Pallas kernels  161 us (98%)
  local copies, waits for them, and re-layouts  3.5 us (2%)
    pallas_call x1, Pallas kernels, shards(): pl.pallas_call(kernel, out_shape=(jax.ShapeDtypeStruct((tokens, ks), BF16...  161 us
    unnamed x2, local copies, waits for them, and re-layouts  3.5 us

profile of v5, /device:TPU:1, one launch (start us, length us, event | category | flops | bytes accessed | tf_op | source)
XLA Modules:
  0.0 164.9 jit_solution(8398063530655693079)
XLA Ops:
  0.6 160.8 %shard_map.68 = (bf16[384,768]{1,0:T(8,128)(2,1)}, f32[48,768]{1,0:T(8,128)}) custom-call(bf16[384,1664]{1,0:T(8,128)(2,1)} %t_ref.1, bf16[1664]{0:T(1024)(128)(2,1)} %g_ref.1, bf16[96,1664]{1,0:T(8,128)(2,1)} %bitcast.1, bf16[384,768]{1,0:T(8,128)(2,1)} %x_ref.1, bf16[3072,768]{1,0:T(8,128)(2,1)} %weight_ref.1), custom_call_target="tpu_custom_call" | custom-call | tf_op jit(solution)/shard_map/pallas_call | solution.py:524
  161.4 1.9 %copy.9 = bf16[384,768]{1,0:T(8,128)(2,1)} copy(bf16[384,768]{1,0:T(8,128)(2,1)} %get-tuple-element.4) | data formatting | bytes 1179648
  163.3 1.6 copy.10

commit v6 on v5

--- a/solution.py
+++ b/solution.py
@@ -19,16 +19,16 @@
 SIBLING = 49
 NARROW_RS = 51
 NARROW_AG = 57
-CORE_SUM = 65
-WIDE_RS = 70
-FINAL = 75
-SLOTS = 79
+CORE_SUM = 67
+WIDE_RS = 73
+FINAL = 79
+SLOTS = 83
 
 
 def kernel(
     t_ref, g_ref, pt_ref, x_ref, weight_ref, ig_ref, wg_ref, window, wt_ref, xt_ref,
     ct, lhs, hid, sq, inverse, part, far_out, near_out, far_in, near_in, m, igacc,
-    kept, core_out, core_in, wide_out, wide_in, fin_out, fin_in, send_sem, recv_sem, local_sem,
+    kept, core_out, core_in, wide_out, wide_in, tile_out, tile_in, far_wide_out, far_wide_in, fin_out, fin_in, send_sem, recv_sem, local_sem,
 ):
     c = lax.axis_index("section")
     w = lax.axis_index("wide")
@@ -340,13 +340,24 @@
 
     lax.fori_loop(0, 8, products, 0)
 
+    tiles = cols // 128
 
     def own_copy(h, e):
         return copy(m.at[n, h], m.at[n, h], NARROW_AG + 2 * e + h, by(e))
 
-    def pass_on(e):
-        piece = m.at[(n + 3 + 2 * e) % 4, e]
-        return copy(piece, piece, NARROW_AG + 4 + e, by(e))
+    def pass_on(e, j):
+        piece = m.at[(n + 3 + 2 * e) % 4, e, j]
+        return copy(piece, piece, NARROW_AG + 4 + tiles * e + j, by(e))
+
+    def pass_all(e):
+        def one(j, carry):
+            pass_on(e, j).start()
+            return carry
+
+        lax.fori_loop(0, tiles, one, 0)
+
+    def whole(b, h):
+        return jnp.concatenate([m[b, h, j] for j in range(tiles)], axis=1)
 
     early_copy(e2).wait_recv()
     late_copy(e2).wait_recv()
@@ -364,7 +375,9 @@
 
         span = pl.ds(pl.multiple_of(cols * h, cols), cols)
         own = part[h] + x_ref[:, span].astype(F32)
-        m[n, h] = (own + near_in[0, h].astype(F32) + near_in[1, h].astype(F32)).astype(BF16)
+        total = (own + near_in[0, h].astype(F32) + near_in[1, h].astype(F32)).astype(BF16)
+        for j in range(tiles):
+            m[n, h, j] = total[:, 128 * j : 128 * j + 128]
         own_copy(h, 0).start()
         own_copy(h, 1).start()
         return carry
@@ -373,30 +386,35 @@
     igacc[...] = jnp.zeros((tokens, ks), F32)
     me = 4 * y + x
 
-    def core_copy(d):
-        return copy(core_out.at[d], core_in.at[d], CORE_SUM + d, sibling)
-
-    def wide_send(d):
+    def core_copy(slot):
+        return copy(core_out.at[slot], core_in.at[slot], CORE_SUM + slot, sibling)
+
+    def core_tile(j):
+        return copy(tile_out.at[j], tile_in.at[j], CORE_SUM + 3 + j, sibling)
+
+    def wide_send(out, into, slot):
         def one(k, carry):
             yy, xx = peer(k)
-            copy(
-                wide_out.at[d, 4 * yy + xx], wide_in.at[d, me], WIDE_RS + d, {"wide": at(zl, yy, xx)}
-            ).start()
+            copy(out.at[4 * yy + xx], into.at[me], slot, {"wide": at(zl, yy, xx)}).start()
             return carry
 
         lax.fori_loop(1, 16, one, 0)
 
-    def wide_all(d):
-        return copy(
-            wide_out.at[d, pl.ds(0, 15)], wide_in.at[d, pl.ds(0, 15)], WIDE_RS + d, {"wide": at(zl, y, (x + 1) % 4)}
-        )
-
-    def chip_sum(d):
-        core_copy(d).wait_recv()
-        both = (kept[...] + core_in[d].astype(F32)).astype(BF16)
-        wide_out[d] = both.reshape(16, half, cols)
-        wide_in[d, me] = wide_out[d, me]
-        wide_send(d)
+    def wide_all(out, into, slot):
+        return copy(out.at[pl.ds(0, 15)], into.at[pl.ds(0, 15)], slot, {"wide": at(zl, y, (x + 1) % 4)})
+
+    def wide_block(slot):
+        return wide_all(wide_out.at[slot], wide_in.at[slot], WIDE_RS + slot)
+
+    def wide_tile(j):
+        return wide_all(far_wide_out.at[j], far_wide_in.at[j], WIDE_RS + 3 + j)
+
+    def chip_sum(slot):
+        core_copy(slot).wait_recv()
+        both = (kept[...] + core_in[slot].astype(F32)).astype(BF16)
+        wide_out[slot] = both.reshape(16, half, cols)
+        wide_in[slot, me] = wide_out[slot, me]
+        wide_send(wide_out.at[slot], wide_in.at[slot], WIDE_RS + slot)
 
     def final_copy(d):
         return pltpu.make_async_remote_copy(
@@ -404,11 +422,12 @@
             recv_sem=recv_sem.at[FINAL + 2 * zl + c], device_id=target(d), device_id_type=MESH,
         )
 
-    def reduce(d):
-        wide_all(d).wait_recv()
-        total = wide_in[d, 0].astype(F32)
+    def reduce(slot):
+        d = jnp.where(slot == 2, 3, slot)
+        wide_block(slot).wait_recv()
+        total = wide_in[slot, 0].astype(F32)
         for k in range(1, 16):
-            total = total + wide_in[d, k].astype(F32)
+            total = total + wide_in[slot, k].astype(F32)
         stays = jnp.logical_and(at_home, d == 0)
 
         @pl.when(stays)
@@ -420,43 +439,50 @@
             fin_out[d] = total.astype(BF16)
             final_copy(d).start()
 
+    def add_input_grad(b, h):
+        block = ct[pl.ds(8 * b + 4 * h, 4), :, pl.ds(kt, ks)].reshape(cols, ks)
+        igacc[...] += jnp.dot(whole(b, h), block, preferred_element_type=F32)
+
+    soon = 1 - n % 2
+
     def backward(i, carry):
-        @pl.when(i == 2)
-        def _():
-            own_copy(0, 0).wait_recv()
-            pass_on(0).start()
-            own_copy(1, 1).wait_recv()
-            pass_on(1).start()
-            own_copy(1, 0).wait_recv()
-
-        @pl.when(i == 4)
-        def _():
-            own_copy(0, 1).wait_recv()
-
-        @pl.when(i == 6)
-        def _():
-            early_waits()
-            pass_on(0).wait_recv()
-            pass_on(1).wait_recv()
-
-        r = i // 2
-        d = jnp.where(r == 0, 0, jnp.where(r == 1, 3, jnp.where(r == 2, 1, 2)))
-        h = jnp.where(i % 2 == 0, 1 - c, c)
+        @pl.when(jnp.logical_or(i == 2, i == 4))
+        def _():
+            arrived = jnp.where(i == 2, soon, 1 - soon)
+            own_copy(arrived, arrived).wait_recv()
+            pass_all(arrived)
+            own_copy(arrived, 1 - arrived).wait_recv()
+
+        d = jnp.where(i < 2, 0, jnp.where(i % 2 == 0, 3, 1))
+        h = jnp.where(i == 0, 1 - c, jnp.where(i == 1, c, jnp.where(i < 4, soon, 1 - soon)))
+        slot = jnp.where(d == 3, 2, d)
         b = (n + d) % 4
-        kept[...] = jnp.dot(xt_ref[...], m[b, h], preferred_element_type=F32)
-
-        @pl.when(i % 2 == 0)
-        def _():
-            core_out[d] = kept[...].astype(BF16)
-            core_copy(d).start()
-
-        block = ct[pl.ds(8 * b + 4 * h, 4), :, pl.ds(kt, ks)].reshape(cols, ks)
-        igacc[...] += jnp.dot(m[b, h], block, preferred_element_type=F32)
-
-        @pl.when(i % 2 == 1)
-        def _():
-            chip_sum(d)
-
+        kept[...] = jnp.dot(xt_ref[...], whole(b, h), preferred_element_type=F32)
+
+        @pl.when(h != c)
+        def _():
+            core_out[slot] = kept[...].astype(BF16)
+            core_copy(slot).start()
+
+        add_input_grad(b, h)
+
+        @pl.when(h == c)
+        def _():
+            chip_sum(slot)
+
+        return carry
+
+    def far_gradient(j, carry):
+        b = (n + 2) % 4
+        for e in range(2):
+            pass_on(e, j).wait_recv()
+        tile_out[j] = jnp.dot(xt_ref[...], m[b, 1 - c, j], preferred_element_type=F32).astype(BF16)
+        core_tile(j).start()
+        own = jnp.dot(xt_ref[...], m[b, c, j], preferred_element_type=F32)
+        core_tile(j).wait_recv()
+        far_wide_out[j] = (own + tile_in[j].astype(F32)).astype(BF16).reshape(16, half, 128)
+        far_wide_in[j, me] = far_wide_out[j, me]
+        wide_send(far_wide_out.at[j], far_wide_in.at[j], WIDE_RS + 3 + j)
         return carry
 
     def early_waits():
@@ -474,25 +500,43 @@
             for k in range(1, 4):
                 weight_copy(k, n // 2).wait_send()
 
-    lax.fori_loop(0, 8, backward, 0)
+    def early_sums(slot, carry):
+        reduce(slot)
+        return carry
+
+    def last_input_grad(h, carry):
+        add_input_grad((n + 2) % 4, h)
+        return carry
+
+    lax.fori_loop(0, 6, backward, 0)
+    early_waits()
+    lax.fori_loop(0, tiles, far_gradient, 0)
+    lax.fori_loop(0, 2, last_input_grad, 0)
     for h in range(2):
         span = slice(cols * h, cols * h + cols)
-        ig_ref[:, span] = (m[n, h].astype(F32) + igacc[:, span]).astype(BF16)
-
-    def reduce_all(r, carry):
-        reduce(jnp.where(r == 1, 3, jnp.where(r == 2, 1, 2 * (r // 3))))
-        return carry
-
-    lax.fori_loop(0, 4, reduce_all, 0)
+        ig_ref[:, span] = (whole(n, h).astype(F32) + igacc[:, span]).astype(BF16)
+
+    lax.fori_loop(0, 3, early_sums, 0)
+    for j in range(tiles):
+        wide_tile(j).wait_recv()
+        total = far_wide_in[j, 0].astype(F32)
+        for k in range(1, 16):
+            total = total + far_wide_in[j, k].astype(F32)
+        fin_out[2, :, 128 * j : 128 * j + 128] = total.astype(BF16)
+    final_copy(2).start()
 
     def late_waits():
         for e in range(2):
-            pass_on(e).wait_send()
+            for j in range(tiles):
+                pass_on(e, j).wait_send()
             for h in range(2):
                 own_copy(h, e).wait_send()
+        for k in range(3):
+            core_copy(k).wait_send()
+            core_tile(k).wait_send()
+            wide_block(k).wait_send()
+            wide_tile(k).wait_send()
         for d in range(4):
-            core_copy(d).wait_send()
-            wide_all(d).wait_send()
 
             @pl.when(jnp.logical_not(jnp.logical_and(at_home, d == 0)))
             def _():
@@ -543,13 +587,17 @@
             pltpu.VMEM((2, 2, tokens, cols), BF16),
             pltpu.VMEM((2, tokens, cols), BF16),
             pltpu.VMEM((2, 2, tokens, cols), BF16),
-            pltpu.VMEM((4, 2, tokens, cols), BF16),
+            pltpu.VMEM((4, 2, cols // 128, tokens, 128), BF16),
             pltpu.VMEM((tokens, ks), F32),
             pltpu.VMEM((ks, cols), F32),
-            pltpu.VMEM((4, ks, cols), BF16),
-            pltpu.VMEM((4, ks, cols), BF16),
-            pltpu.VMEM((4, 16, half, cols), BF16),
-            pltpu.VMEM((4, 16, half, cols), BF16),
+            pltpu.VMEM((3, ks, cols), BF16),
+            pltpu.VMEM((3, ks, cols), BF16),
+            pltpu.VMEM((3, 16, half, cols), BF16),
+            pltpu.VMEM((3, 16, half, cols), BF16),
+            pltpu.VMEM((3, ks, 128), BF16),
+            pltpu.VMEM((3, ks, 128), BF16),
+            pltpu.VMEM((3, 16, half, 128), BF16),
+            pltpu.VMEM((3, 16, half, 128), BF16),
             pltpu.VMEM((4, half, cols), BF16),
             pltpu.VMEM((2, 2, half, cols), BF16),
             pltpu.SemaphoreType.DMA((SLOTS,)),

time: 165 us -> 161 us (0.976)
  Pallas kernels: 161 us -> 157 us
    pallas_call x1, Pallas kernels: 161 us -> 157 us  [shards(): pl.pallas_call(kernel, out_shape=(jax.ShapeDtypeStruct((tokens, ks), BF16...]
where the time goes in v6:
time: 161 us
  Pallas kernels  157 us (98%)
  local copies, waits for them, and re-layouts  3.5 us (2%)
    pallas_call x1, Pallas kernels, shards(): pl.pallas_call(kernel, out_shape=(jax.ShapeDtypeStruct((tokens, ks), BF16...  157 us
    unnamed x2, local copies, waits for them, and re-layouts  3.5 us

profile of v6, /device:TPU:1, one launch (start us, length us, event | category | flops | bytes accessed | tf_op | source)
XLA Modules:
  0.0 160.8 jit_solution(12906790680382173773)
XLA Ops:
  0.6 156.6 %shard_map.68 = (bf16[384,768]{1,0:T(8,128)(2,1)}, f32[48,768]{1,0:T(8,128)}) custom-call(bf16[384,1664]{1,0:T(8,128)(2,1)} %t_ref.1, bf16[1664]{0:T(1024)(128)(2,1)} %g_ref.1, bf16[96,1664]{1,0:T(8,128)(2,1)} %bitcast.1, bf16[384,768]{1,0:T(8,128)(2,1)} %x_ref.1, bf16[3072,768]{1,0:T(8,128)(2,1)} %weight_ref.1), custom_call_target="tpu_custom_call" | custom-call | tf_op jit(solution)/shard_map/pallas_call | solution.py:568
  157.3 1.9 %copy.9 = bf16[384,768]{1,0:T(8,128)(2,1)} copy(bf16[384,768]{1,0:T(8,128)(2,1)} %get-tuple-element.4) | data formatting | bytes 1179648
  159.2 1.6 copy.10

commit v7 on v6

--- a/solution.py
+++ b/solution.py
@@ -89,8 +89,6 @@
         def _():
             pl.semaphore_signal(barrier, inc=1, device_id=device, device_id_type=MESH)
 
-    pl.semaphore_wait(barrier, jnp.where(at_home, len(greeted) + 18, len(greeted) + 19))
-
     def copy(src, dst, slot, device):
         return pltpu.make_async_remote_copy(
             src_ref=src, dst_ref=dst, send_sem=send_sem.at[slot], recv_sem=recv_sem.at[slot],
@@ -106,8 +104,6 @@
         )
 
     ct[w, rows, p_cols] = pt_ref[rows, :]
-    z_copy = copy(ct.at[w, rows, p_cols], ct.at[w, rows, p_cols], ZSWAP, z_other)
-    z_copy.start()
 
     @pl.when(holder)
     def _():
@@ -124,9 +120,28 @@
             return carry
 
         lax.fori_loop(0, 4, transpose, 0)
+        ct[w_slab, rows, w_cols] = wt_ref[n]
+
+    eye = lax.broadcasted_iota(jnp.int32, (128, 128), 0) == lax.broadcasted_iota(jnp.int32, (128, 128), 1)
+    groups = tokens // 128
+    sq[0] = jnp.zeros((8, 128), F32)
+
+    def squares(i, carry):
+        part_t = t_ref[pl.ds(pl.multiple_of(128 * i, 128), 128), :].astype(F32)
+        col = jnp.sum(part_t * part_t, axis=1, keepdims=True)
+        sq[0, pl.ds(i, 1), :] = jnp.sum(jnp.where(eye, col, 0.0), axis=0, keepdims=True)
+        return carry
+
+    lax.fori_loop(0, groups, squares, 0)
+    pl.semaphore_wait(barrier, jnp.where(at_home, len(greeted) + 18, len(greeted) + 19))
+
+    z_copy = copy(ct.at[w, rows, p_cols], ct.at[w, rows, p_cols], ZSWAP, z_other)
+    z_copy.start()
+
+    @pl.when(holder)
+    def _():
         for k in (2, 1, 3):
             weight_copy(k, n // 2).start()
-        ct[w_slab, rows, w_cols] = wt_ref[n]
 
     def weight_arrives(plane):
         @pl.when(n != 2 * plane + y // 2)
@@ -222,17 +237,6 @@
     near_plane, far_plane = Plane(0, p_first), Plane(1, 1 - p_first)
     near_plane.begin()
 
-    eye = lax.broadcasted_iota(jnp.int32, (128, 128), 0) == lax.broadcasted_iota(jnp.int32, (128, 128), 1)
-    groups = tokens // 128
-    sq[0] = jnp.zeros((8, 128), F32)
-
-    def squares(i, carry):
-        part_t = t_ref[pl.ds(pl.multiple_of(128 * i, 128), 128), :].astype(F32)
-        col = jnp.sum(part_t * part_t, axis=1, keepdims=True)
-        sq[0, pl.ds(i, 1), :] = jnp.sum(jnp.where(eye, col, 0.0), axis=0, keepdims=True)
-        return carry
-
-    lax.fori_loop(0, groups, squares, 0)
     sq_copies = [copy(sq.at[0], sq.at[d], SQUARES + d - 1, n_dev[d]) for d in (1, 2, 3)]
     for item in sq_copies:
         item.start()
@@ -259,10 +263,10 @@
     near_plane.first_far()
     near_plane.second_near(1)
     near_plane.second_far(0)
-    far_plane.begin()
     near_plane.second_near(2)
     near_plane.second_far(1)
     near_plane.second_near(3)
+    far_plane.begin()
     far_plane.first_near()
     near_plane.second_far(2)
     near_plane.second_far(3)
@@ -524,18 +528,18 @@
             total = total + far_wide_in[j, k].astype(F32)
         fin_out[2, :, 128 * j : 128 * j + 128] = total.astype(BF16)
     final_copy(2).start()
+    for e in range(2):
+        for j in range(tiles):
+            pass_on(e, j).wait_send()
+        for h in range(2):
+            own_copy(h, e).wait_send()
+    for k in range(3):
+        core_copy(k).wait_send()
+        core_tile(k).wait_send()
+        wide_block(k).wait_send()
+        wide_tile(k).wait_send()
 
     def late_waits():
-        for e in range(2):
-            for j in range(tiles):
-                pass_on(e, j).wait_send()
-            for h in range(2):
-                own_copy(h, e).wait_send()
-        for k in range(3):
-            core_copy(k).wait_send()
-            core_tile(k).wait_send()
-            wide_block(k).wait_send()
-            wide_tile(k).wait_send()
         for d in range(4):
 
             @pl.when(jnp.logical_not(jnp.logical_and(at_home, d == 0)))

time: 161 us -> 159 us (0.988)
  Pallas kernels: 157 us -> 154 us
    pallas_call x1, Pallas kernels: 157 us -> 154 us  [shards(): pl.pallas_call(kernel, out_shape=(jax.ShapeDtypeStruct((tokens, ks), BF16...]
where the time goes in v7:
time: 159 us
  Pallas kernels  154 us (97%)
  local copies, waits for them, and re-layouts  3.5 us (2%)
    pallas_call x1, Pallas kernels, shards(): pl.pallas_call(kernel, out_shape=(jax.ShapeDtypeStruct((tokens, ks), BF16...  154 us
    unnamed x2, local copies, waits for them, and re-layouts  3.5 us

profile of v7, /device:TPU:1, one launch (start us, length us, event | category | flops | bytes accessed | tf_op | source)
XLA Modules:
  0.0 158.5 jit_solution(7170657022579282164)
XLA Ops:
  0.6 154.4 %shard_map.68 = (bf16[384,768]{1,0:T(8,128)(2,1)}, f32[48,768]{1,0:T(8,128)}) custom-call(bf16[384,1664]{1,0:T(8,128)(2,1)} %t_ref.1, bf16[1664]{0:T(1024)(128)(2,1)} %g_ref.1, bf16[96,1664]{1,0:T(8,128)(2,1)} %bitcast.1, bf16[384,768]{1,0:T(8,128)(2,1)} %x_ref.1, bf16[3072,768]{1,0:T(8,128)(2,1)} %weight_ref.1), custom_call_target="tpu_custom_call" | custom-call | tf_op jit(solution)/shard_map/pallas_call | solution.py:572
  155.0 1.9 %copy.9 = bf16[384,768]{1,0:T(8,128)(2,1)} copy(bf16[384,768]{1,0:T(8,128)(2,1)} %get-tuple-element.4) | data formatting | bytes 1179648
  156.9 1.6 copy.10

commit v8 on v7

--- a/solution.py
+++ b/solution.py
@@ -313,14 +313,17 @@
             far_plane.second_far(1)
             far_plane.second_near(3)
 
-        @pl.when(jnp.logical_or(i == 4, i == 6))
-        def _():
-            send_late(jnp.where(i == 4, e1, e2))
-
         @pl.when(i == 4)
         def _():
             far_plane.second_far(2)
             far_plane.second_far(3)
+
+        @pl.when(jnp.logical_or(i == 4, i == 6))
+        def _():
+            send_late(jnp.where(i == 4, e1, e2))
+
+        @pl.when(i == 4)
+        def _():
             far_plane.whole().wait_recv()
 
         e = jnp.where(r == 1, e1, e2)

time: 159 us -> 158 us (level)
  no operation moved by 1% of the time
where the time goes in v8:
time: 158 us
  Pallas kernels  154 us (97%)
  local copies, waits for them, and re-layouts  3.5 us (2%)
    pallas_call x1, Pallas kernels, shards(): pl.pallas_call(kernel, out_shape=(jax.ShapeDtypeStruct((tokens, ks), BF16...  154 us
    unnamed x2, local copies, waits for them, and re-layouts  3.5 us

profile of v8, /device:TPU:1, one launch (start us, length us, event | category | flops | bytes accessed | tf_op | source)
XLA Modules:
  0.0 158.2 jit_solution(7111663005618214560)
XLA Ops:
  0.6 154.1 %shard_map.68 = (bf16[384,768]{1,0:T(8,128)(2,1)}, f32[48,768]{1,0:T(8,128)}) custom-call(bf16[384,1664]{1,0:T(8,128)(2,1)} %t_ref.1, bf16[1664]{0:T(1024)(128)(2,1)} %g_ref.1, bf16[96,1664]{1,0:T(8,128)(2,1)} %bitcast.1, bf16[384,768]{1,0:T(8,128)(2,1)} %x_ref.1, bf16[3072,768]{1,0:T(8,128)(2,1)} %weight_ref.1), custom_call_target="tpu_custom_call" | custom-call | tf_op jit(solution)/shard_map/pallas_call | solution.py:575
  154.7 1.9 %copy.9 = bf16[384,768]{1,0:T(8,128)(2,1)} copy(bf16[384,768]{1,0:T(8,128)(2,1)} %get-tuple-element.4) | data formatting | bytes 1179648
  156.6 1.6 copy.10
